TPU v7x, 32 devices: a whole 2x2x4 slice. The times are simulated.
32 devices in a mesh: replica: 4 (over y, x), shard: 2 (over core), ctx: 4 (over z).
Axes of the slice: x: 2, y: 2, z: 4, core: 2. Of those that a mesh axis runs over, the one named last changes fastest.
Arguments:
- tokens: bfloat16 [16, 1024, 768], P(('replica', 'shard'), 'ctx'), may hold values from -6 to 6
- query_key_value_weight: bfloat16 [768, 2304], P(('shard', 'ctx')), may hold values from -0.21875 to 0.21875
- attention_output_weight: bfloat16 [768, 768], P(('shard', 'ctx')), may hold values from -1.75 to 1.75
- expansion_matrix: bfloat16 [768, 3072], P(('shard', 'ctx')), may hold values from -0.21875 to 0.21875
- feedforward_output_weight: bfloat16 [3072, 768], P(('shard', 'ctx')), may hold values from -0.109375 to 0.109375
- norm_gains: bfloat16 [2, 768], P(None, ('shard', 'ctx')), may hold values from 0.099609375 to 1.8984375
- norm_biases: bfloat16 [2, 768], P(None, ('shard', 'ctx')), may hold values from -3 to 3
- projection_bias_set: bfloat16 [4, 768], P(None, ('shard', 'ctx')), may hold values from -3 to 3
- expansion_offset_vector: bfloat16 [3072], P(('shard', 'ctx')), may hold values from -3 to 3
- cotangent: bfloat16 [16, 1024, 768], P(('replica', 'shard'), 'ctx'), may hold values from -6 to 6
Outputs:
- output: bfloat16 [16, 1024, 768], P(('replica', 'shard'), 'ctx')
- grad_tokens: bfloat16 [16, 1024, 768], P(('replica', 'shard'), 'ctx')
- grad_w_qkv: float32 [768, 2304], P(('shard', 'ctx'))
- grad_w_out: float32 [768, 768], P(('shard', 'ctx'))
- grad_w_in: float32 [768, 3072], P(('shard', 'ctx'))
- grad_w_ffout: float32 [3072, 768], P(('shard', 'ctx'))
- grad_norm_gains: float32 [2, 768], P(None, ('shard', 'ctx'))
- grad_norm_biases: float32 [2, 768], P(None, ('shard', 'ctx'))
- grad_proj_biases: float32 [4, 768], P(None, ('shard', 'ctx'))
- grad_ff_bias: float32 [3072], P(('shard', 'ctx'))
All inputs are finite; a program needn't handle non-finite values.
Results may differ from a plain program's by a relative error of at most 0.03.
Values may be sent and summed in bfloat16 or wider, within the bound.
No kernel may reach another device: no remote copies, remote signals or barrier semaphores. Data moves between devices by JAX's collectives and lax.ppermute only.
A program may use at most 256 MiB of HBM per device.

v0:
```python
import jax
import jax.numpy as jnp
from jax import lax
from jax.sharding import PartitionSpec as P

HEADS = 12
HEAD_DIM = 64


EPS = 1e-05
NEG = -1e30


def normalize(values):
    deviation_from_average = values - jnp.mean(values, -1, keepdims=True)
    spread = lax.rsqrt(
        jnp.mean(deviation_from_average * deviation_from_average, -1, keepdims=True) + EPS
    )
    return (deviation_from_average * spread, spread)


def norm_back(upstream, normed, spread):
    first_mean = jnp.mean(upstream, -1, keepdims=True)
    second_mean = jnp.mean(upstream * normed, -1, keepdims=True)
    return spread * (upstream - first_mean - normed * second_mean)


def split_heads(matrix):
    return matrix.reshape(matrix.shape[0], HEADS, HEAD_DIM)


def masked_scores(query_heads, key_heads, query_pos, key_pos):
    scores = jnp.einsum("qhe,khe->hqk", query_heads, key_heads, preferred_element_type=jnp.float32)
    return jnp.where(key_pos[None, None, :] <= query_pos[None, :, None], scores, NEG)


def body(
    tokens,
    query_key_value_weight,
    attention_output_weight,
    expansion_matrix,
    feedforward_output_weight,
    norm_gains,
    norm_biases,
    projection_bias_set,
    expansion_offset_vector,
    cotangent,
):
    seq_count, span_len, width = tokens.shape
    row_count = seq_count * span_len
    seq_len = span_len * lax.axis_size("ctx")
    scale = HEAD_DIM ** (-0.5)
    query_pos = lax.axis_index("ctx") * span_len + jnp.arange(span_len, dtype=jnp.int32)
    key_pos = jnp.arange(seq_len, dtype=jnp.int32)
    qkv_full, out_full, gains_low, shifts_low, biases_low = (
        lax.all_gather(query_key_value_weight, ("shard", "ctx"), axis=0, tiled=True),
        lax.all_gather(attention_output_weight, ("shard", "ctx"), axis=0, tiled=True),
        lax.all_gather(norm_gains, ("shard", "ctx"), axis=1, tiled=True),
        lax.all_gather(norm_biases, ("shard", "ctx"), axis=1, tiled=True),
        lax.all_gather(projection_bias_set, ("shard", "ctx"), axis=1, tiled=True),
    )
    gains = gains_low.astype(jnp.float32)
    shifts = shifts_low.astype(jnp.float32)
    biases = biases_low.astype(jnp.float32)
    inputs = tokens.reshape(row_count, width).astype(jnp.float32)
    normed_one, spread_one = normalize(inputs)
    first_input_rows = (normed_one * gains[0] + shifts[0]).astype(jnp.bfloat16)
    output_projected = jnp.dot(first_input_rows, qkv_full, preferred_element_type=jnp.float32)
    queries = (
        ((output_projected[:, :width] + biases[0]) * scale)
        .astype(jnp.bfloat16)
        .reshape(seq_count, span_len, width)
    )
    keys = (
        output_projected[:, width : 2 * width]
        .astype(jnp.bfloat16)
        .reshape(seq_count, span_len, width)
    )
    values = (
        (output_projected[:, 2 * width :] + biases[1])
        .astype(jnp.bfloat16)
        .reshape(seq_count, span_len, width)
    )
    whole_keys, whole_values = (
        lax.all_gather(keys, "ctx", axis=1, tiled=True),
        lax.all_gather(values, "ctx", axis=1, tiled=True),
    )

    def attend(items):
        query_rows, key_rows, value_rows = items
        scores = masked_scores(split_heads(query_rows), split_heads(key_rows), query_pos, key_pos)
        highest = jnp.max(scores, -1, keepdims=True)
        weights = jnp.exp(scores - highest)
        totals = jnp.sum(weights, -1, keepdims=True)
        probs_low = (weights / totals).astype(jnp.bfloat16)
        mixed_rows = jnp.einsum(
            "hqk,khe->qhe", probs_low, split_heads(value_rows), preferred_element_type=jnp.float32
        )
        return (mixed_rows.reshape(query_rows.shape[0], width), (highest + jnp.log(totals))[..., 0])

    attention_mixed, log_totals = lax.map(attend, (queries, whole_keys, whole_values))
    mixed_low = attention_mixed.reshape(row_count, width).astype(jnp.bfloat16)
    hidden_input_rows = (
        inputs + jnp.dot(mixed_low, out_full, preferred_element_type=jnp.float32) + biases[2]
    )
    in_full, back_full, inner_low = (
        lax.all_gather(expansion_matrix, ("shard", "ctx"), axis=0, tiled=True),
        lax.all_gather(feedforward_output_weight, ("shard", "ctx"), axis=0, tiled=True),
        lax.all_gather(expansion_offset_vector, ("shard", "ctx"), axis=0, tiled=True),
    )
    normed_two, spread_two = normalize(hidden_input_rows)
    latter_operand_lines = (normed_two * gains[1] + shifts[1]).astype(jnp.bfloat16)
    expanded_activation = jnp.dot(
        latter_operand_lines, in_full, preferred_element_type=jnp.float32
    ) + inner_low.astype(jnp.float32)
    activated_hidden = jax.nn.gelu(expanded_activation).astype(jnp.bfloat16)
    result = (
        hidden_input_rows
        + jnp.dot(activated_hidden, back_full, preferred_element_type=jnp.float32)
        + biases[3]
    )
    output = result.astype(jnp.bfloat16).reshape(seq_count, span_len, width)
    in_full, back_full, inner_low = (
        lax.all_gather(expansion_matrix, ("shard", "ctx"), axis=0, tiled=True),
        lax.all_gather(feedforward_output_weight, ("shard", "ctx"), axis=0, tiled=True),
        lax.all_gather(expansion_offset_vector, ("shard", "ctx"), axis=0, tiled=True),
    )
    qkv_full, out_full, gains_low, shifts_low, biases_low = (
        lax.all_gather(query_key_value_weight, ("shard", "ctx"), axis=0, tiled=True),
        lax.all_gather(attention_output_weight, ("shard", "ctx"), axis=0, tiled=True),
        lax.all_gather(norm_gains, ("shard", "ctx"), axis=1, tiled=True),
        lax.all_gather(norm_biases, ("shard", "ctx"), axis=1, tiled=True),
        lax.all_gather(projection_bias_set, ("shard", "ctx"), axis=1, tiled=True),
    )
    gains = gains_low.astype(jnp.float32)
    whole_keys, whole_values = (
        lax.all_gather(keys, "ctx", axis=1, tiled=True),
        lax.all_gather(values, "ctx", axis=1, tiled=True),
    )
    grad_low = cotangent.reshape(row_count, width)
    grad_rows = grad_low.astype(jnp.float32)
    grad_last_bias = jnp.sum(grad_rows, 0)
    grad_back_w = jnp.dot(activated_hidden.T, grad_low, preferred_element_type=jnp.float32)
    grad_active = jnp.dot(grad_low, back_full.T, preferred_element_type=jnp.float32)
    grad_inner = jax.vjp(jax.nn.gelu, expanded_activation)[1](grad_active)[0].astype(jnp.bfloat16)
    grad_inner_bias = jnp.sum(grad_inner.astype(jnp.float32), 0)
    grad_in_w = jnp.dot(latter_operand_lines.T, grad_inner, preferred_element_type=jnp.float32)
    grad_second = jnp.dot(grad_inner, in_full.T, preferred_element_type=jnp.float32)
    grad_gain_two = jnp.sum(grad_second * normed_two, 0)
    grad_shift_two = jnp.sum(grad_second, 0)
    grad_hidden = grad_rows + norm_back(grad_second * gains[1], normed_two, spread_two)
    grad_branch = grad_hidden.astype(jnp.bfloat16)
    grad_out_bias = jnp.sum(grad_branch.astype(jnp.float32), 0)
    grad_out_w = jnp.dot(mixed_low.T, grad_branch, preferred_element_type=jnp.float32)
    grad_mixed = (
        jnp.dot(grad_branch, out_full.T, preferred_element_type=jnp.float32)
        .astype(jnp.bfloat16)
        .reshape(seq_count, span_len, width)
    )

    def query_terms(query_rows, key_rows, value_rows, grad_rows_low, log_rows):
        query_heads = split_heads(query_rows)
        key_heads = split_heads(key_rows)
        grad_heads = split_heads(grad_rows_low)
        scores = masked_scores(query_heads, key_heads, query_pos, key_pos)
        probs = jnp.exp(scores - log_rows[:, :, None])
        grad_probs = jnp.einsum(
            "qhe,khe->hqk", grad_heads, split_heads(value_rows), preferred_element_type=jnp.float32
        )
        level = jnp.sum(probs * grad_probs, -1)
        grad_scores = (probs * (grad_probs - level[:, :, None])).astype(jnp.bfloat16)
        grad_query = jnp.einsum(
            "hqk,khe->qhe", grad_scores, key_heads, preferred_element_type=jnp.float32
        )
        return (probs, grad_scores, level, grad_query.reshape(query_rows.shape[0], width))

    def rows_and_keys(items):
        query_rows, key_rows, value_rows, grad_rows_low, log_rows = items
        probs, grad_scores, level, grad_query = query_terms(
            query_rows, key_rows, value_rows, grad_rows_low, log_rows
        )
        grad_key = jnp.einsum(
            "hqk,qhe->khe", grad_scores, split_heads(query_rows), preferred_element_type=jnp.float32
        )
        grad_value = jnp.einsum(
            "hqk,qhe->khe",
            probs.astype(jnp.bfloat16),
            split_heads(grad_rows_low),
            preferred_element_type=jnp.float32,
        )
        return (
            grad_query,
            jnp.concatenate(
                [grad_key.reshape(seq_len, width), grad_value.reshape(seq_len, width)], -1
            ),
        )

    grad_queries, key_terms = lax.map(
        rows_and_keys, (queries, whole_keys, whole_values, grad_mixed, log_totals)
    )
    key_grad = lax.psum_scatter(
        key_terms.astype(jnp.bfloat16), "ctx", scatter_dimension=1, tiled=True
    ).astype(jnp.float32)
    grad_query_low = grad_queries.reshape(row_count, width).astype(jnp.bfloat16)
    grad_kv_low = key_grad.reshape(row_count, 2 * width).astype(jnp.bfloat16)
    grad_query_scaled = grad_query_low.astype(jnp.float32) * scale
    grad_projected = jnp.concatenate([grad_query_scaled.astype(jnp.bfloat16), grad_kv_low], 1)
    grad_query_bias = jnp.sum(grad_query_scaled, 0)
    grad_value_bias = jnp.sum(grad_kv_low[:, width:].astype(jnp.float32), 0)
    grad_qkv_w = jnp.dot(first_input_rows.T, grad_projected, preferred_element_type=jnp.float32)
    grad_first = jnp.dot(grad_projected, qkv_full.T, preferred_element_type=jnp.float32)
    grad_gain_one = jnp.sum(grad_first * normed_one, 0)
    grad_shift_one = jnp.sum(grad_first, 0)
    grad_inputs = grad_hidden + norm_back(grad_first * gains[0], normed_one, spread_one)
    grad_tokens = grad_inputs.astype(jnp.bfloat16).reshape(seq_count, span_len, width)
    grad_gains = jnp.stack([grad_gain_one, grad_gain_two])
    grad_shifts = jnp.stack([grad_shift_one, grad_shift_two])
    offset_derivatives = jnp.stack(
        [grad_query_bias, grad_value_bias, grad_out_bias, grad_last_bias]
    )
    owned_qkv, owned_out, owned_gains, owned_shifts, owned_biases = (
        lax.psum_scatter(grad_qkv_w, ("shard", "ctx"), scatter_dimension=0, tiled=True),
        lax.psum_scatter(grad_out_w, ("shard", "ctx"), scatter_dimension=0, tiled=True),
        lax.psum_scatter(grad_gains, ("shard", "ctx"), scatter_dimension=1, tiled=True),
        lax.psum_scatter(grad_shifts, ("shard", "ctx"), scatter_dimension=1, tiled=True),
        lax.psum_scatter(offset_derivatives, ("shard", "ctx"), scatter_dimension=1, tiled=True),
    )
    owned_in, owned_back, owned_inner = (
        lax.psum_scatter(grad_in_w, ("shard", "ctx"), scatter_dimension=0, tiled=True),
        lax.psum_scatter(grad_back_w, ("shard", "ctx"), scatter_dimension=0, tiled=True),
        lax.psum_scatter(grad_inner_bias, ("shard", "ctx"), scatter_dimension=0, tiled=True),
    )
    summed = (
        lax.psum(owned_qkv.astype(jnp.bfloat16), "replica").astype(jnp.float32),
        lax.psum(owned_out.astype(jnp.bfloat16), "replica").astype(jnp.float32),
        lax.psum(owned_in.astype(jnp.bfloat16), "replica").astype(jnp.float32),
        lax.psum(owned_back.astype(jnp.bfloat16), "replica").astype(jnp.float32),
        lax.psum(owned_gains.astype(jnp.bfloat16), "replica").astype(jnp.float32),
        lax.psum(owned_shifts.astype(jnp.bfloat16), "replica").astype(jnp.float32),
        lax.psum(owned_biases.astype(jnp.bfloat16), "replica").astype(jnp.float32),
        lax.psum(owned_inner.astype(jnp.bfloat16), "replica").astype(jnp.float32),
    )
    return (
        output,
        grad_tokens,
        summed[0],
        summed[1],
        summed[2],
        summed[3],
        summed[4],
        summed[5],
        summed[6],
        summed[7],
    )


def solution(mesh):
    placed = (
        P(("replica", "shard"), "ctx", None),
        P(("shard", "ctx"), None),
        P(("shard", "ctx"), None),
        P(("shard", "ctx"), None),
        P(("shard", "ctx"), None),
        P(None, ("shard", "ctx")),
        P(None, ("shard", "ctx")),
        P(None, ("shard", "ctx")),
        P(("shard", "ctx")),
        P(("replica", "shard"), "ctx", None),
    )
    return jax.shard_map(
        body,
        mesh=mesh,
        in_specs=placed,
        out_specs=(
            P(("replica", "shard"), "ctx", None),
            P(("replica", "shard"), "ctx", None),
            P(("shard", "ctx"), None),
            P(("shard", "ctx"), None),
            P(("shard", "ctx"), None),
            P(("shard", "ctx"), None),
            P(None, ("shard", "ctx")),
            P(None, ("shard", "ctx")),
            P(None, ("shard", "ctx")),
            P(("shard", "ctx")),
        ),
        check_vma=False,
    )
```

profile of v0, /device:TPU:9, one launch (start us, length us, event | category | flops | bytes accessed | tf_op | source)
XLA Modules:
  0.0 1280.5 jit_solution(4981000468089560295)
XLA Ops:
  10.8 13.9 %all-gather = bf16[8,96,2]{1,2,0:T(2,128)(2,1)S(1)} all-gather(bf16[1,96,2]{1,2,0:T(2,128)(2,1)} %bitcast.226), channel_id=1, replica_groups=mesh['replica'=4,'shard'=2,'ctx'=4] {'shard','ctx'}, dimensions={0}, use_global_device_ids=true | all-gather | bytes 3456 | tf_op jit(solution)/shard_map/all_gather | solution.py:58
  24.8 15.8 %all-gather.1 = bf16[8,96,2]{1,2,0:T(2,128)(2,1)S(1)} all-gather(bf16[1,96,2]{1,2,0:T(2,128)(2,1)} %bitcast.227), channel_id=1, replica_groups=mesh['replica'=4,'shard'=2,'ctx'=4] {'shard','ctx'}, dimensions={0}, use_global_device_ids=true | all-gather | bytes 3456 | tf_op jit(solution)/shard_map/all_gather | solution.py:59
  42.9 8.8 all-gather.11.cloned.1.call-done
  59.2 14.3 %all-gather.2 = bf16[8,96,4]{1,2,0:T(4,128)(2,1)S(1)} all-gather(bf16[1,96,4]{1,2,0:T(4,128)(2,1)S(1)} %bitcast.225), channel_id=1, replica_groups=mesh['replica'=4,'shard'=2,'ctx'=4] {'shard','ctx'}, dimensions={0}, use_global_device_ids=true | all-gather | bytes 6912 | tf_op jit(solution)/shard_map/all_gather | solution.py:60
  79.4 33.6 %all-gather.3 = bf16[8,1,384]{2,1,0:T(2,128)(2,1)S(1)} all-gather(bf16[1,1,384]{2,1,0:T(2,128)(2,1)S(1)} %reshape.259), channel_id=1, replica_groups=mesh['replica'=4,'shard'=2,'ctx'=4] {'shard','ctx'}, dimensions={0}, use_global_device_ids=true | all-gather | bytes 6912 | tf_op jit(solution)/shard_map/all_gather | solution.py:109
  119.8 63.8 %all-gather.13.cloned.1.call-done = bf16[2,1024,768]{1,2,0:T(8,128)(2,1)} async-done(((bf16[2,256,768]{1,2,0:T(8,128)(2,1)}), bf16[2,1024,768]{1,2,0:T(8,128)(2,1)}) %all-gather.13.cloned.1.call-update) | async-done | bytes 3145744 | tf_op jit(solution)/shard_map/all_gather | solution.py:86
  183.6 27.0 %while.26 = (s32[]{:T(128)}, bf16[2,256,768]{2,1,0:T(8,128)(2,1)S(1)}, f32[2,12,256]{2,1,0:T(8,128)}, bf16[2,1024,768]{1,2,0:T(8,128)(2,1)}, bf16[2,256,768]{1,2...) while((s32[]{:T(128)}, bf16[2,256,768]{2,1,0:T(8,128)(2,1)S(1)}, ...), condition=%wide.region_5.6_spmd.clone, body=%wide.region_2.5_spmd.clone.sunk | while | flops 833877248 | bytes 51484784 | solution.py:101
  213.4 47.1 %all-gather.19.cloned.1.call-done = bf16[768,3072]{1,0:T(8,128)(2,1)} async-done(((bf16[96,3072]{1,0:T(8,128)(2,1)}), bf16[768,3072]{1,0:T(8,128)(2,1)}) %all-gather.19.cloned.1.call-update) | async-done | bytes 4718608 | tf_op jit(solution)/shard_map/all_gather | solution.py:107
  267.6 44.9 %all-gather.21.cloned.1.call-done = bf16[3072,768]{1,0:T(8,128)(2,1)} async-done(((bf16[384,768]{1,0:T(8,128)(2,1)}), bf16[3072,768]{1,0:T(8,128)(2,1)}) %all-gather.21.cloned.1.call-update) | async-done | bytes 4718608 | tf_op jit(solution)/shard_map/all_gather | solution.py:108
  312.5 10.0 convert_reduce_fusion
  331.1 74.3 %while.27 = (s32[]{:T(128)}, bf16[2,256,768]{2,1,0:T(8,128)(2,1)}, bf16[2,1024,1536]{2,1,0:T(8,128)(2,1)}, bf16[2,1024,768]{1,2,0:T(8,128)(2,1)}, bf16[2,256,768...) while((s32[]{:T(128)}, bf16[2,256,768]{2,1,0:T(8,128)(2,1)}, ...), condition=%wide.region_12.13_spmd.clone, body=%wide.region_10.12_spmd.clone.sunk | while | flops 2057565440 | bytes 134437008 | solution.py:198
  378.5 7.2 multiply_reduce_fusion.7
  409.6 10.4 fusion.56
  430.1 86.1 %reduce-scatter.15.cloned.1.call-done = bf16[2,256,1536]{2,1,0:T(8,128)(2,1)} async-done(((bf16[2,1024,1536]{2,1,0:T(8,128)(2,1)}), bf16[2,256,1536]{2,1,0:T(8,128)(2,1)}) %reduce-scatter.15.cloned.1.call-update) | async-done | bytes 1572880 | tf_op jit(solution)/shard_map/reduce_scatter | solution.py:201
  536.0 30.1 %all-reduce = bf16[3072]{0:T(1024)(128)(2,1)S(1)} all-reduce(f32[3072]{0:T(1024)S(1)} %copy-done.28), channel_id=10, replica_groups=mesh['replica'=4,'shard'=2,'ctx'=4] {'shard','ctx'}, use_global_device_ids=true, to_apply=%region_39.40.clone | all-reduce | flops 3072 | bytes 18432
  574.4 187.8 %reduce-scatter.23.cloned.1.call-done = f32[384,768]{1,0:T(8,128)} async-done(((f32[3072,768]{1,0:T(8,128)}), f32[384,768]{1,0:T(8,128)}) %reduce-scatter.23.cloned.1.call-update) | async-done | bytes 1179664 | tf_op jit(solution)/shard_map/reduce_scatter | solution.py:230
  764.4 187.6 %reduce-scatter.21.cloned.1.call-done = f32[96,3072]{1,0:T(8,128)} async-done(((f32[768,3072]{1,0:T(8,128)}), f32[96,3072]{1,0:T(8,128)}) %reduce-scatter.21.cloned.1.call-update) | async-done | bytes 1179664 | tf_op jit(solution)/shard_map/reduce_scatter | solution.py:229
  954.2 141.4 %reduce-scatter.17.cloned.1.call-done = f32[96,2304]{1,0:T(8,128)} async-done(((f32[768,2304]{1,0:T(8,128)}), f32[96,2304]{1,0:T(8,128)}) %reduce-scatter.17.cloned.1.call-update) | async-done | bytes 884752 | tf_op jit(solution)/shard_map/reduce_scatter | solution.py:222
  1097.6 9.6 add_convert_fusion
  1108.6 21.6 %reduce-scatter.27.cloned.1.call-done = f32[96,2]{1,0:T(8,128)} async-done(((f32[768,2]{1,0:T(8,128)}), f32[96,2]{1,0:T(8,128)}) %reduce-scatter.27.cloned.1.call-update) | async-done | bytes 784
  1131.1 32.5 %reduce-scatter.25.cloned.1.call-done = f32[96,2]{1,0:T(8,128)} async-done(((f32[768,2]{1,0:T(8,128)}), f32[96,2]{1,0:T(8,128)}) %reduce-scatter.25.cloned.1.call-update) | async-done | bytes 784
  1164.4 31.9 %reduce-scatter.29.cloned.1.call-done = f32[96,4]{1,0:T(8,128)} async-done(((f32[768,4]{1,0:T(8,128)}), f32[96,4]{1,0:T(8,128)}) %reduce-scatter.29.cloned.1.call-update) | async-done | bytes 1552
  1197.2 8.1 all-reduce.1
  1207.6 59.3 %all-reduce.5.cloned.1.call-done = (bf16[96,2304]{1,0:T(8,128)(2,1)}, bf16[96,768]{1,0:T(8,128)(2,1)}, bf16[96,3072]{1,0:T(8,128)(2,1)}, bf16[384,768]{1,0:T(8,128)(2,1)}) async-done(((bf16[96,2304]{1,0:T(8,128)(2,1)}, bf16[96,768]{1,0:T(8,128)(2,1)}, bf16[96,3072]{1,0:T(8,128)(2,1)}, bf16[384,768]{1,0:T(8,128)(2,1)}), (bf16[96,2304]{1,0:T(8,128)(2,1)}, bf16[96,768]{1,0:T(8,128)(2,1)}, ...) | async-done | bytes 1769488 | tf_op jit(solution)/shard_map/psum | solution.py:234
  (248 shorter events, 199.2 us)
Async XLA Ops:
  7.2 44.6 %all-gather.11.cloned.1.call-start = ((), (), s32[]{:S(2)}) async-start(), calls=%async_computation.8 | async-start | bytes 3981312 | tf_op jit(solution)/shard_map/all_gather | solution.py:56
  7.9 111.8 %all-gather.15.cloned.1.call-start = ((), (), s32[]{:S(2)}) async-start(), calls=%async_computation.10 | async-start | bytes 3932160 | tf_op jit(solution)/shard_map/all_gather | solution.py:85
  9.3 42.4 %copy-start.17 = (f32[1,2,2,128]{3,1,2,0:T(2,128)}, f32[1,2,2,128]{3,1,2,0:T(2,128)S(1)}, u32[]{:S(2)}) copy-start(f32[1,2,2,128]{3,1,2,0:T(2,128)S(1)} %copy.88) | copy-start | bytes 6148
  40.8 285.2 %copy-start.23 = (f32[768]{0:T(1024)}, f32[768]{0:T(1024)S(1)}, u32[]{:S(2)}) copy-start(f32[768]{0:T(1024)S(1)} %get-tuple-element.226) | copy-start | bytes 9220
  59.1 124.4 %all-gather.13.cloned.1.call-start = ((), (), s32[]{:S(2)}) async-start(), calls=%async_computation.9 | async-start | bytes 3932160 | tf_op jit(solution)/shard_map/all_gather | solution.py:86
  77.5 133.1 %all-gather.17.cloned.1.call-start = ((), (), s32[]{:S(2)}) async-start(), calls=%async_computation.11 | async-start | bytes 1327104 | tf_op jit(solution)/shard_map/all_gather | solution.py:57
  78.1 182.4 %all-gather.19.cloned.1.call-start = ((), (), s32[]{:S(2)}) async-start(), calls=%async_computation.12 | async-start | bytes 5308416 | tf_op jit(solution)/shard_map/all_gather | solution.py:107
  78.7 233.8 %all-gather.21.cloned.1.call-start = ((), (), s32[]{:S(2)}) async-start(), calls=%async_computation.13 | async-start | bytes 5308416 | tf_op jit(solution)/shard_map/all_gather | solution.py:108
  79.3 437.0 %reduce-scatter.15.cloned.1.call-start = ((), (), s32[]{:S(2)}) async-start(), calls=%async_computation.14 | async-start | bytes 7864320 | tf_op jit(solution)/shard_map/reduce_scatter | solution.py:201
  112.9 199.6 %copy-start.26 = (f32[8,1,384]{2,1,0:T(1,128)}, f32[8,1,384]{2,1,0:T(1,128)S(1)}, u32[]{:S(2)}) copy-start(f32[8,1,384]{2,1,0:T(1,128)S(1)} %convert_element_type.206) | copy-start | bytes 36868
  213.0 113.0 %copy-start.4 = (f32[512,768]{1,0:T(8,128)}, f32[512,768]{1,0:T(8,128)S(1)}, u32[]{:S(2)}) copy-start(f32[512,768]{1,0:T(8,128)S(1)} %get-tuple-element.289) | copy-start | bytes 4718596
  213.1 113.0 %copy-start.21 = (f32[512]{0:T(512)}, f32[512]{0:T(512)S(1)}, u32[]{:S(2)}) copy-start(f32[512]{0:T(512)S(1)} %broadcast_multiply_fusion.4) | copy-start | bytes 6148
  213.4 112.7 %copy-start.29 = (f32[512]{0:T(512)}, f32[512]{0:T(512)S(1)}, u32[]{:S(2)}) copy-start(f32[512]{0:T(512)S(1)} %add_rsqrt_fusion) | copy-start | bytes 6148
  260.5 52.0 %copy-start.11 = (bf16[2,256,768]{2,1,0:T(8,128)(2,1)S(1)}, bf16[2,256,768]{2,1,0:T(8,128)(2,1)}, u32[]{:S(2)}) copy-start(bf16[2,256,768]{2,1,0:T(8,128)(2,1)} %param.23) | copy-start | bytes 2359300
  405.4 167.4 %reduce-scatter.19.cloned.1.call-start = ((), (), s32[]{:S(2)}) async-start(), calls=%async_computation.16 | async-start | bytes 2654208 | tf_op jit(solution)/shard_map/reduce_scatter | solution.py:223
  409.2 353.1 %reduce-scatter.23.cloned.1.call-start = ((), (), s32[]{:S(2)}) async-start(), calls=%async_computation.18 | async-start | bytes 10616832 | tf_op jit(solution)/shard_map/reduce_scatter | solution.py:230
  420.1 532.0 %reduce-scatter.21.cloned.1.call-start = ((), (), s32[]{:S(2)}) async-start(), calls=%async_computation.17 | async-start | bytes 10616832 | tf_op jit(solution)/shard_map/reduce_scatter | solution.py:229
  428.6 87.6 %copy-start.8 = (bf16[512,768]{1,0:T(8,128)(2,1)S(1)}, bf16[512,768]{1,0:T(8,128)(2,1)}, u32[]{:S(2)}) copy-start(bf16[512,768]{1,0:T(8,128)(2,1)} %copy-done.7) | copy-start | bytes 2359300
  428.6 666.9 %reduce-scatter.17.cloned.1.call-start = ((), (), s32[]{:S(2)}) async-start(), calls=%async_computation.15 | async-start | bytes 7962624 | tf_op jit(solution)/shard_map/reduce_scatter | solution.py:222
  522.7 607.6 %reduce-scatter.27.cloned.1.call-start = ((), (), s32[]{:S(2)}) async-start(), calls=%async_computation.20 | async-start | bytes 442368
  532.6 631.0 %reduce-scatter.25.cloned.1.call-start = ((), (), s32[]{:S(2)}) async-start(), calls=%async_computation.19 | async-start | bytes 442368
  533.7 662.6 %reduce-scatter.29.cloned.1.call-start = ((), (), s32[]{:S(2)}) async-start(), calls=%async_computation.21 | async-start | bytes 442368
  534.7 732.2 %all-reduce.5.cloned.1.call-start = ((), (), s32[]{:S(2)}) async-start(), calls=%async_computation.22 | async-start | bytes 3538944 | tf_op jit(solution)/shard_map/psum | solution.py:234
  574.4 523.2 %copy-start.31 = (f32[768]{0:T(1024)S(1)}, f32[768]{0:T(1024)}, u32[]{:S(2)}) copy-start(f32[768]{0:T(1024)} %get-tuple-element.222) | copy-start | bytes 9220
  (32 other events, 164.8 us)
Sparse Core Ops, SparseCore 0:
  9.6 42.0 all-gather.10
  59.3 60.4 all-gather.14
  121.9 61.5 all-gather.12
  185.0 24.0 all-gather.16
  210.5 49.9 all-gather.18
  262.0 50.5 all-gather.20
  405.5 110.7 reduce-scatter.14
  518.6 54.1 reduce-scatter.18
  575.1 187.1 reduce-scatter.22
  764.4 187.5 reduce-scatter.20
  954.4 141.1 reduce-scatter.16
  1097.7 32.4 reduce-scatter.26
  1132.6 30.9 reduce-scatter.24
  1165.7 30.5 reduce-scatter.28
  1200.6 66.2 all-reduce.4
where the time goes:
time: 1290 us; the launch traced here: 1280 us
  waiting for transfers between devices  928 us (72%)
  blocking collectives  116 us (9%)
  matrix products  113 us (9%)
  other arithmetic  56.8 us (4%)
  local copies, waits for them, and re-layouts  51.2 us (4%)
  between operations  15.4 us (1%)
    reduce_scatter x1, waiting for transfers between devices, body(): lax.psum_scatter(grad_back_w, ('shard', 'ctx'), scatter_dimension=0, tile...  188 us
    reduce_scatter x1, waiting for transfers between devices, body(): lax.psum_scatter(grad_in_w, ('shard', 'ctx'), scatter_dimension=0, tiled=...  188 us
    reduce_scatter x1, waiting for transfers between devices, body(): lax.psum_scatter(grad_qkv_w, ('shard', 'ctx'), scatter_dimension=0, tiled...  141 us
    unnamed x18, waiting for transfers between devices  88.4 us
    reduce_scatter x1, waiting for transfers between devices, body(): lax.psum_scatter(key_terms.astype(jnp.bfloat16), 'ctx', scatter_dimension...  86.1 us
    all_gather x1, waiting for transfers between devices, body(): lax.all_gather(values, 'ctx', axis=1, tiled=True)  63.8 us
    psum x1, waiting for transfers between devices, body(): lax.psum(owned_qkv.astype(jnp.bfloat16), 'replica').astype(jnp.float32)  59.3 us
    all_gather x1, waiting for transfers between devices, body(): lax.all_gather(expansion_matrix, ('shard', 'ctx'), axis=0, tiled=True)  47.1 us
  transfers between devices with their start and end apart: 15, of which 14 were waited for; matrix products, arithmetic and copies ran while one was open for 9% of the time, Pallas kernels for 0%

commit v1 on v0

v1 whole, which is shorter than its diff:
```python
import functools

import jax
import jax.numpy as jnp
from jax import lax
from jax.experimental import pallas as pl
from jax.experimental.pallas import tpu as pltpu
from jax.sharding import PartitionSpec as P

HEADS = 12
HEAD_DIM = 64
EPS = 1e-05
NEG = -1e30
BLOCK = 256
LINE = ("shard", "ctx")
EVERY = ("replica", "shard", "ctx")
BF = jnp.bfloat16
F32 = jnp.float32


def normalize(values):
    centered = values - jnp.mean(values, -1, keepdims=True)
    spread = lax.rsqrt(jnp.mean(centered * centered, -1, keepdims=True) + EPS)
    return centered * spread, spread


def norm_back(upstream, normed, spread):
    first_mean = jnp.mean(upstream, -1, keepdims=True)
    second_mean = jnp.mean(upstream * normed, -1, keepdims=True)
    return spread * (upstream - first_mean - normed * second_mean)


def dot(a, b):
    return jnp.dot(a, b, preferred_element_type=F32)


def dot_nt(a, b):
    return lax.dot_general(a, b, (((1,), (1,)), ((), ())), preferred_element_type=F32)


def dot_tn(a, b):
    return lax.dot_general(a, b, (((0,), (0,)), ((), ())), preferred_element_type=F32)


def place(rank, block, rows):
    per_rank = rows // BLOCK
    owner, part = block // per_rank, block % per_rank
    return pl.multiple_of((owner ^ rank) * rows + part * BLOCK, BLOCK)


def head_mask(lanes, head):
    lane = lax.broadcasted_iota(jnp.int32, (BLOCK, lanes), 1)
    return (lane >= head * HEAD_DIM) & (lane < (head + 1) * HEAD_DIM)


def diagonal(scores):
    key = lax.broadcasted_iota(jnp.int32, scores.shape, 0)
    query = lax.broadcasted_iota(jnp.int32, scores.shape, 1)
    return jnp.where(key <= query, scores, NEG)


def attend_kernel(rows, rank_ref, qkv_ref, mixed_ref, log_ref, keys, values_t):
    length, lanes = mixed_ref.shape
    rank = rank_ref[0]
    heads = lanes // HEAD_DIM
    for block in range(length // BLOCK):
        at = pl.ds(place(rank, block, rows), BLOCK)
        here = slice(block * BLOCK, (block + 1) * BLOCK)
        keys[here, :] = qkv_ref[at, lanes : 2 * lanes]
        values_t[:, here] = qkv_ref[at, 2 * lanes :].T
    for block in range(length // BLOCK):
        at = pl.ds(place(rank, block, rows), BLOCK)
        start, stop = block * BLOCK, (block + 1) * BLOCK
        query = qkv_ref[at, :lanes]
        parts = []
        for head in range(heads):
            one = slice(head * HEAD_DIM, (head + 1) * HEAD_DIM)
            one_query = jnp.where(head_mask(lanes, head), query, jnp.zeros_like(query))
            near = diagonal(dot_nt(keys[start:stop, :], one_query))
            highest = jnp.max(near, 0, keepdims=True)
            if block:
                far = dot_nt(keys[:start, :], one_query)
                highest = jnp.maximum(highest, jnp.max(far, 0, keepdims=True))
            near = jnp.exp(near - highest)
            total = jnp.sum(near, 0, keepdims=True)
            mixed = dot(values_t[one, start:stop], near.astype(BF))
            if block:
                far = jnp.exp(far - highest)
                total = total + jnp.sum(far, 0, keepdims=True)
                mixed = mixed + dot(values_t[one, :start], far.astype(BF))
            parts.append(mixed / total)
            log_ref[head : head + 1, start:stop] = highest + jnp.log(total)
        mixed_ref[at, :] = jnp.concatenate(parts, 0).T.astype(BF)


def attend_back_kernel(
    rows, rank_ref, qkv_ref, grad_ref, log_ref, out_ref, keys, values, keys_t, key_sum, value_sum
):
    length, lanes = grad_ref.shape
    rank = rank_ref[0]
    heads = lanes // HEAD_DIM
    scale = HEAD_DIM ** (-0.5)
    for block in range(length // BLOCK):
        at = pl.ds(place(rank, block, rows), BLOCK)
        here = slice(block * BLOCK, (block + 1) * BLOCK)
        key = qkv_ref[at, lanes : 2 * lanes]
        keys[here, :] = key
        keys_t[:, here] = key.T
        values[here, :] = qkv_ref[at, 2 * lanes :]
    for block in range(length // BLOCK):
        at = pl.ds(place(rank, block, rows), BLOCK)
        start, stop = block * BLOCK, (block + 1) * BLOCK
        query = qkv_ref[at, :lanes]
        grad = grad_ref[at, :]
        parts = []
        near_key = near_value = far_key = far_value = None
        for head in range(heads):
            one = slice(head * HEAD_DIM, (head + 1) * HEAD_DIM)
            mask = head_mask(lanes, head)
            one_query = jnp.where(mask, query, jnp.zeros_like(query))
            one_grad = jnp.where(mask, grad, jnp.zeros_like(grad))
            logs = log_ref[head : head + 1, start:stop]
            near = jnp.exp(diagonal(dot_nt(keys[start:stop, :], one_query)) - logs)
            near_grad = dot_nt(values[start:stop, :], one_grad)
            level = jnp.sum(near * near_grad, 0, keepdims=True)
            if block:
                far = jnp.exp(dot_nt(keys[:start, :], one_query) - logs)
                far_grad = dot_nt(values[:start, :], one_grad)
                level = level + jnp.sum(far * far_grad, 0, keepdims=True)
            near_low = near.astype(BF)
            near_scores = (near * (near_grad - level)).astype(BF)
            value_term, key_term = dot(near_low, one_grad), dot(near_scores, one_query)
            near_value = value_term if near_value is None else near_value + value_term
            near_key = key_term if near_key is None else near_key + key_term
            query_term = dot(keys_t[one, start:stop], near_scores)
            if block:
                far_low = far.astype(BF)
                far_scores = (far * (far_grad - level)).astype(BF)
                value_term, key_term = dot(far_low, one_grad), dot(far_scores, one_query)
                far_value = value_term if far_value is None else far_value + value_term
                far_key = key_term if far_key is None else far_key + key_term
                query_term = query_term + dot(keys_t[one, :start], far_scores)
            parts.append(query_term)
        key_sum[start:stop, :] = near_key
        value_sum[start:stop, :] = near_value
        if block:
            key_sum[:start, :] += far_key
            value_sum[:start, :] += far_value
        query_grad = jnp.concatenate(parts, 0).T.astype(BF).astype(F32) * scale
        out_ref[at, :lanes] = query_grad.astype(BF)
    for block in range(length // BLOCK):
        at = pl.ds(place(rank, block, rows), BLOCK)
        here = slice(block * BLOCK, (block + 1) * BLOCK)
        out_ref[at, lanes : 2 * lanes] = key_sum[here, :].astype(BF)
        out_ref[at, 2 * lanes :] = value_sum[here, :].astype(BF)


def attention_calls(length, rows, groups, lanes):
    heads = lanes // HEAD_DIM
    wide = pl.BlockSpec((length, 3 * lanes), lambda g, r: (0, g))
    thin = pl.BlockSpec((length, lanes), lambda g, r: (0, g))
    logs = pl.BlockSpec((None, heads, length), lambda g, r: (g, 0, 0))
    pairs = groups * heads * length * length // 2
    params = pltpu.CompilerParams(vmem_limit_bytes=56 * 2**20)
    forward = pl.pallas_call(
        functools.partial(attend_kernel, rows),
        grid_spec=pltpu.PrefetchScalarGridSpec(
            num_scalar_prefetch=1,
            grid=(groups,),
            in_specs=[wide],
            out_specs=[thin, logs],
            scratch_shapes=[pltpu.VMEM((length, lanes), BF), pltpu.VMEM((lanes, length), BF)],
        ),
        out_shape=[
            jax.ShapeDtypeStruct((length, groups * lanes), BF),
            jax.ShapeDtypeStruct((groups, heads, length), F32),
        ],
        cost_estimate=pl.CostEstimate(
            flops=pairs * 16 * HEAD_DIM, bytes_accessed=length * groups * lanes * 8, transcendentals=pairs
        ),
        compiler_params=params,
        name="attend",
    )
    backward = pl.pallas_call(
        functools.partial(attend_back_kernel, rows),
        grid_spec=pltpu.PrefetchScalarGridSpec(
            num_scalar_prefetch=1,
            grid=(groups,),
            in_specs=[wide, thin, logs],
            out_specs=wide,
            scratch_shapes=[
                pltpu.VMEM((length, lanes), BF),
                pltpu.VMEM((length, lanes), BF),
                pltpu.VMEM((lanes, length), BF),
                pltpu.VMEM((length, lanes), F32),
                pltpu.VMEM((length, lanes), F32),
            ],
        ),
        out_shape=jax.ShapeDtypeStruct((length, 3 * groups * lanes), BF),
        cost_estimate=pl.CostEstimate(
            flops=pairs * 40 * HEAD_DIM, bytes_accessed=length * groups * lanes * 14, transcendentals=pairs
        ),
        compiler_params=params,
        name="attend_back",
    )
    return forward, backward


def row_moves(shards, spans, seqs):
    chips = spans // (2 * seqs)
    moves = ([], [])
    for shard in range(shards):
        for span in range(spans):
            for item in range(seqs):
                sequence = (shard % 2) * seqs + item
                rank = span // seqs
                target = (shard - shard % 2 + rank % 2) * spans + sequence * chips + rank // 2
                moves[(item + span) % 2].append((shard * spans + span, target))
    return moves


def back_moves(moves):
    return tuple([(b, a) for a, b in one] for one in moves)


def group_moves(shards, spans, ranks):
    chips = ranks // 2
    moves = []
    for k in range(1, ranks):
        one = []
        for shard in range(shards):
            for span in range(spans):
                rank = (span % chips) * 2 + shard % 2
                other = rank ^ k
                target = (shard - shard % 2 + other % 2) * spans + span - span % chips + other // 2
                one.append((shard * spans + span, target))
        moves.append(one)
    return moves


def body(
    tokens, weight_qkv, weight_out, weight_in, weight_back, gains_in, shifts_in, biases_in, ff_bias_in, cotangent
):
    seqs, span, width = tokens.shape
    shards, spans = lax.axis_size("shard"), lax.axis_size("ctx")
    shard, ctx = lax.axis_index("shard"), lax.axis_index("ctx")
    ranks = spans // seqs
    rows, length = seqs * span, spans * span
    chips = ranks // 2
    rank = (ctx % chips) * 2 + shard % 2
    core = shard % 2
    hidden = weight_back.shape[0] * shards * spans
    part, ff_part = width // ranks, hidden // ranks
    blocks = shards * spans
    heads = HEADS // ranks
    lanes = 2 * HEAD_DIM if heads % 2 == 0 else heads * HEAD_DIM
    groups = part // lanes
    scale = HEAD_DIM ** (-0.5)
    moves = row_moves(shards, spans, seqs)
    returns = back_moves(moves)
    turns = group_moves(shards, spans, ranks)
    odd_span = ctx % 2
    odd_sequence = (ctx // chips) % 2
    paired = shards == 2

    def to_rows(items):
        one = lax.ppermute(lax.dynamic_index_in_dim(items, odd_span, 0, False), LINE, moves[0])
        two = lax.ppermute(lax.dynamic_index_in_dim(items, 1 - odd_span, 0, False), LINE, moves[1])
        return jnp.where(odd_sequence == 0, jnp.concatenate([one, two]), jnp.concatenate([two, one]))

    def from_rows(low):
        items = low.reshape(seqs, span, width)
        one = lax.ppermute(lax.dynamic_index_in_dim(items, odd_sequence, 0, False), LINE, returns[0])
        two = lax.ppermute(lax.dynamic_index_in_dim(items, 1 - odd_sequence, 0, False), LINE, returns[1])
        return jnp.where(odd_span == 0, jnp.stack([one, two]), jnp.stack([two, one]))

    def gather_rows(low):
        return jnp.concatenate([low] + [lax.ppermute(low, LINE, one) for one in turns])

    def scatter_rows(partial):
        total = partial[:rows]
        for k, one in enumerate(turns):
            sent = partial[(k + 1) * rows : (k + 2) * rows].astype(BF)
            total = total + lax.ppermute(sent, LINE, one).astype(F32)
        return total

    def swap(items):
        return lax.ppermute(items, "shard", [(0, 1), (1, 0)])

    def gather_columns(weight):
        if not paired:
            whole = lax.all_gather(weight, LINE, axis=0, tiled=True)
            return lax.dynamic_index_in_dim(whole, rank, 1, False)
        mine = lax.dynamic_index_in_dim(weight, core, 1, False)
        other = swap(lax.dynamic_index_in_dim(weight, 1 - core, 1, False))
        both = jnp.where(core == 0, jnp.stack([mine, other]), jnp.stack([other, mine]))
        whole = lax.all_gather(both, "ctx", axis=1)
        return whole.reshape(blocks * weight.shape[0], weight.shape[2])

    def gather_lines(weight):
        if not paired:
            whole = lax.all_gather(weight, LINE, axis=0, tiled=True)
            size = whole.shape[0] // ranks
            return lax.dynamic_slice_in_dim(whole, rank * size, size, 0)
        return lax.all_gather(weight, "ctx", axis=0, tiled=True)

    def scatter_columns(grad):
        low = grad.astype(BF)
        if not paired:
            whole = jnp.zeros((grad.shape[0], ranks, grad.shape[1]), BF)
            whole = lax.dynamic_update_slice_in_dim(whole, low[:, None], rank, 1)
            owned = lax.psum_scatter(whole, LINE, scatter_dimension=0, tiled=True)
            return lax.psum(owned, "replica").astype(F32)
        both = low.reshape(2, spans, -1, grad.shape[1]).swapaxes(0, 1)
        owned = lax.psum_scatter(both, "ctx", scatter_dimension=0, tiled=True)[0]
        owned = lax.psum(owned, "replica")
        mine = lax.dynamic_index_in_dim(owned, core, 0, False)
        other = swap(lax.dynamic_index_in_dim(owned, 1 - core, 0, False))
        mine, other = mine.astype(F32), other.astype(F32)
        return jnp.where(core == 0, jnp.stack([mine, other], 1), jnp.stack([other, mine], 1))

    def scatter_lines(grad):
        low = grad.astype(BF)
        if not paired:
            whole = jnp.zeros((grad.shape[0] * ranks, grad.shape[1]), BF)
            whole = lax.dynamic_update_slice_in_dim(whole, low, rank * grad.shape[0], 0)
            owned = lax.psum_scatter(whole, LINE, scatter_dimension=0, tiled=True)
        else:
            owned = lax.psum_scatter(low, "ctx", scatter_dimension=0, tiled=True)
        return lax.psum(owned, "replica").astype(F32)

    small_in = jnp.concatenate(
        [gains_in, shifts_in, biases_in, ff_bias_in.reshape(hidden // width, width // blocks)]
    )
    small = lax.all_gather(small_in, LINE, axis=0).astype(F32)
    vectors = small[:, :8].swapaxes(0, 1).reshape(8, width)
    gains, shifts, biases = vectors[0:2], vectors[2:4], vectors[4:8]
    ff_bias = lax.dynamic_slice_in_dim(small[:, 8:].reshape(hidden), rank * ff_part, ff_part, 0)

    local = weight_qkv.shape[0]
    ordered = weight_qkv.reshape(local, 3, ranks, groups, lanes).transpose(0, 2, 3, 1, 4)
    qkv_part = gather_columns(ordered.reshape(local, ranks, 3 * part))
    out_part = gather_lines(weight_out)
    in_part = gather_columns(weight_in.reshape(local, ranks, ff_part))
    back_part = gather_lines(weight_back)

    def of_rank(vector):
        return lax.dynamic_slice_in_dim(vector, rank * part, part, 0).reshape(groups, lanes)

    none = jnp.zeros((groups, lanes), F32)
    qkv_bias = jnp.stack([of_rank(biases[0]), none, of_rank(biases[1])], 1).reshape(-1)
    qkv_scale = jnp.stack([none + scale, none + 1, none + 1], 1).reshape(-1)
    attend, attend_back = attention_calls(length, rows, groups, lanes)
    rank_word = rank.astype(jnp.int32).reshape(1)

    inputs = to_rows(tokens).astype(F32)
    grad_low = to_rows(cotangent)
    normed_one, spread_one = normalize(inputs)
    first_all = gather_rows((normed_one * gains[0] + shifts[0]).astype(BF))
    qkv = ((dot(first_all, qkv_part) + qkv_bias) * qkv_scale).astype(BF)
    mixed, logs = attend(rank_word, qkv)
    hidden_in = inputs + scatter_rows(dot(mixed, out_part)) + biases[2]
    normed_two, spread_two = normalize(hidden_in)
    second_all = gather_rows((normed_two * gains[1] + shifts[1]).astype(BF))
    inner = dot(second_all, in_part) + ff_bias
    active = jax.nn.gelu(inner).astype(BF)
    result = hidden_in + scatter_rows(dot(active, back_part)) + biases[3]
    output = from_rows(result.astype(BF))

    grad_rows = grad_low.astype(F32)
    grad_all = gather_rows(grad_low)
    grad_active = dot_nt(grad_all, back_part)
    grad_inner = jax.vjp(jax.nn.gelu, inner)[1](grad_active)[0].astype(BF)
    grad_back = dot_tn(active, grad_all)
    grad_in = dot_tn(second_all, grad_inner)
    grad_second = scatter_rows(dot_nt(grad_inner, in_part))
    grad_hidden = grad_rows + norm_back(grad_second * gains[1], normed_two, spread_two)

    grad_branch = grad_hidden.astype(BF)
    branch_all = gather_rows(grad_branch)
    grad_mixed = dot_nt(branch_all, out_part).astype(BF)
    grad_out = dot_tn(mixed, branch_all)
    grad_qkv = attend_back(rank_word, qkv, grad_mixed, logs)
    grad_first = scatter_rows(dot_nt(grad_qkv, qkv_part))
    grad_weight = dot_tn(first_all, grad_qkv)
    grad_inputs = grad_hidden + norm_back(grad_first * gains[0], normed_one, spread_one)
    grad_tokens = from_rows(grad_inputs.astype(BF))

    owned_back = scatter_lines(grad_back)
    owned_in = scatter_columns(grad_in).reshape(local, hidden)
    owned_out = scatter_lines(grad_out)
    owned_qkv = scatter_columns(grad_weight).reshape(local, ranks, groups, 3, lanes)
    owned_qkv = owned_qkv.transpose(0, 3, 1, 2, 4).reshape(local, 3 * width)

    qkv_sums = jnp.sum(grad_qkv.astype(F32), 0).reshape(groups, 3, lanes)

    def at_rank(vector, size):
        return lax.dynamic_update_slice_in_dim(jnp.zeros((size,), F32), vector, rank * vector.shape[0], 0)

    sums = jnp.stack(
        [
            jnp.sum(grad_first * normed_one, 0),
            jnp.sum(grad_second * normed_two, 0),
            jnp.sum(grad_first, 0),
            jnp.sum(grad_second, 0),
            at_rank(qkv_sums[:, 0].reshape(part), width),
            at_rank(qkv_sums[:, 2].reshape(part), width),
            jnp.sum(grad_branch.astype(F32), 0),
            jnp.sum(grad_rows, 0),
        ]
    )
    ff_sums = at_rank(jnp.sum(grad_inner.astype(F32), 0), hidden)
    sums = lax.psum((sums, ff_sums), EVERY)
    at = shard * spans + ctx
    mine = lax.dynamic_slice_in_dim(sums[0], at * (width // blocks), width // blocks, 1)
    ff_mine = lax.dynamic_slice_in_dim(sums[1], at * (hidden // blocks), hidden // blocks, 0)
    return (
        output,
        grad_tokens,
        owned_qkv,
        owned_out,
        owned_in,
        owned_back,
        mine[0:2],
        mine[2:4],
        mine[4:8],
        ff_mine,
    )


def solution(mesh):
    rows = P(("replica", "shard"), "ctx", None)
    lines, columns, flat = P(LINE, None), P(None, LINE), P(LINE)
    return jax.shard_map(
        body,
        mesh=mesh,
        in_specs=(rows, lines, lines, lines, lines, columns, columns, columns, flat, rows),
        out_specs=(rows, rows, lines, lines, lines, lines, columns, columns, columns, flat),
        check_vma=False,
    )
```

time: 1290 us -> 553 us (0.43)
  waiting for transfers between devices: 928 us -> 228 us
  matrix products: 113 us -> 58.1 us
  Pallas kernels: 0 us -> 29.8 us
  other arithmetic: 56.8 us -> 28.1 us
  starting transfers between devices: 1.01 us -> 26.1 us
  local copies, waits for them, and re-layouts: 51.2 us -> 32.2 us
    reduce_scatter x5 -> x3, waiting for transfers between devices: 610 us -> 102 us  [the longest x2 61.3 us: scatter_lines(): owned = lax.psum_scatter(low, 'ctx', scatter_dimension=0, tiled=True)]
    all_gather x6 -> x3, waiting for transfers between devices: 170 us -> 0.02 us  [the longest x2 0.01 us: gather_columns(): whole = lax.all_gather(both, 'ctx', axis=1)]
    ppermute x0 -> x20, waiting for transfers between devices: none -> 107 us  [the longest x2 26.5 us: from_rows(): lax.ppermute(lax.dynamic_index_in_dim(items, odd_sequence, 0, False), LIN...]
    unnamed x18 -> x9, waiting for transfers between devices: 88.4 us -> 0.15 us
    dot_general x26 -> x12, matrix products: 113 us -> 58.1 us  [the longest x4 22.2 us: dot(): return jnp.dot(a, b, preferred_element_type=F32)]
    psum x1, waiting for transfers between devices: 59.3 us -> 19 us  [scatter_columns(): owned = lax.psum(owned, 'replica')]
    psum x1, blocking collectives: 8.13 us -> 41.1 us  [body(): sums = lax.psum((sums, ff_sums), EVERY)]
    unnamed x1 -> x0, blocking collectives: 30.1 us -> none
  transfers between devices with their start and end apart: 15 -> 28, of which waited for: 14 -> 12; matrix products, arithmetic and copies ran while one was open for 9% -> 17% of each run, Pallas kernels for 0% -> 5%
where the time goes in v1:
time: 553 us; the launch traced here: 543 us
  waiting for transfers between devices  228 us (41%)
  blocking collectives  125 us (23%)
  matrix products  58.1 us (11%)
  local copies, waits for them, and re-layouts  32.2 us (6%)
  Pallas kernels  29.8 us (5%)
  other arithmetic  28.1 us (5%)
  starting transfers between devices  26.1 us (5%)
  between operations  15.1 us (3%)
    all_gather x1, blocking collectives, body(): small = lax.all_gather(small_in, LINE, axis=0).astype(F32)  61.4 us
    reduce_scatter x2, waiting for transfers between devices, scatter_lines(): owned = lax.psum_scatter(low, 'ctx', scatter_dimension=0, tiled=True)  61.3 us
    psum x1, blocking collectives, body(): sums = lax.psum((sums, ff_sums), EVERY)  41.1 us
    reduce_scatter x1, waiting for transfers between devices, scatter_columns(): owned = lax.psum_scatter(both, 'ctx', scatter_dimension=0, tiled=True)[0]  40.8 us
    ppermute x2, waiting for transfers between devices, from_rows(): lax.ppermute(lax.dynamic_index_in_dim(items, odd_sequence, 0, False), LIN...  26.5 us
    ppermute x2, waiting for transfers between devices, from_rows(): lax.ppermute(lax.dynamic_index_in_dim(items, 1 - odd_sequence, 0, False),...  25.3 us
    ppermute x2, waiting for transfers between devices, to_rows(): lax.ppermute(lax.dynamic_index_in_dim(items, 1 - odd_span, 0, False), LIN...  24.9 us
    ppermute x2, waiting for transfers between devices, to_rows(): lax.ppermute(lax.dynamic_index_in_dim(items, odd_span, 0, False), LINE, m...  24.5 us
  transfers between devices with their start and end apart: 28, of which 12 were waited for; matrix products, arithmetic and copies ran while one was open for 17% of the time, Pallas kernels for 5%

profile of v1, /device:TPU:9, one launch (start us, length us, event | category | flops | bytes accessed | tf_op | source)
XLA Modules:
  0.0 542.7 jit_solution(8196554960706487476)
XLA Ops:
  16.8 4.5 collective-permute-start
  21.5 61.4 %all-gather.1 = bf16[8,12,96]{2,1,0:T(8,128)(2,1)S(1)} all-gather(bf16[1,12,96]{2,1,0:T(8,128)(2,1)S(1)} %maximum_bitcast_fusion), channel_id=2, replica_groups=mesh['replica'=4,'shard'=2,'ctx'=4] {'shard','ctx'}, dimensions={0}, use_global_device_ids=true | all-gather | bytes 20736 | tf_op jit(solution)/shard_map/all_gather | solution.py:335
  86.6 22.7 %all_gather.23 = bf16[384,768]{1,0:T(8,128)(2,1)S(1)} all-gather(bf16[96,768]{1,0:T(8,128)(2,1)S(1)} %copy-done.23), channel_id=1, replica_groups=mesh['replica'=4,'shard'=2,'ctx'=4] {'ctx'}, dimensions={0}, use_global_device_ids=true | all-gather | bytes 737280 | tf_op jit(solution)/shard_map/all_gather | solution.py:305
  109.3 5.5 %multiply_convert_fusion.1.qkv_ref = bf16[1024,1152]{1,0:T(8,128)(2,1)} fusion(bf16[768,1152]{1,0:T(8,128)(2,1)} %bitcast.118, f32[1152]{0:T(1024)S(1)} %copy-done.39, f32[1152]{0:T(1024)S(1)} %add.201, bf16[512,768]{1,0:T(8,128)(2,1)} %collective-permute-done.2, bf16[512,768]{1,0:T(8,128)(2,1)S(1)} %fusion.14), kind=kOutput, calls=%fused_computation.12 | convolution fusion | flops 1818624000 | bytes 5710848 | tf_op jit(solution)/shard_map/dot_general | solution.py:34
  114.9 12.4 %attend.1 = (bf16[1024,384]{1,0:T(8,128)(2,1)}, f32[3,2,1024]{2,1,0:T(2,128)}) custom-call(s32[1]{0:T(128)} %bitcast.2.rank_ref, bf16[1024,1152]{1,0:T(8,128)(2,1)} %multiply_convert_fusion.1.qkv_ref), custom_call_target="tpu_custom_call" | custom-call | flops 3221225472 | bytes 3145728 | tf_op jit(solution)/shard_map/attend/pallas_call | solution.py:361
  138.3 4.6 collective-permute-start.10
  148.0 24.5 %collective-permute-done.10 = bf16[256,768]{1,0:T(8,128)(2,1)S(1)} collective-permute-done((bf16[256,768]{1,0:T(8,128)(2,1)S(1)}, bf16[256,768]{1,0:T(8,128)(2,1)S(1)}, u32[]{:S(2)}, u32[]{:S(2)}) %collective-permute-start.10) | collective-permute-done | bytes 393248 | tf_op jit(solution)/shard_map/ppermute | solution.py:267
  172.5 24.9 %collective-permute-done.11 = bf16[256,768]{1,0:T(8,128)(2,1)} collective-permute-done((bf16[256,768]{1,0:T(8,128)(2,1)S(1)}, bf16[256,768]{1,0:T(8,128)(2,1)}, u32[]{:S(2)}, u32[]{:S(2)}) %collective-permute-start.11) | collective-permute-done | bytes 393248 | tf_op jit(solution)/shard_map/ppermute | solution.py:268
  199.4 9.4 %multiply_convert_fusion = (bf16[1024,1536]{1,0:T(8,128)(2,1)}, f32[1024,1536]{1,0:T(8,128)}) fusion(f32[1536]{0:T(1024)} %dynamic_slice.76, bf16[768,1536]{1,0:T(8,128)(2,1)} %bitcast.116, bf16[512,768]{1,0:T(8,128)(2,1)} %collective-permute-done.5, bf16[512,768]{1,0:T(8,128)(2,1)} %add_convert_fusion), kind=kOutput, calls=%fused_computation.10 | convolution fusion | flops 2434793472 | bytes 13375488 | tf_op jit(solution)/shard_map/dot_general | solution.py:34
  208.8 9.5 %convert_reduce_fusion = (f32[1536]{0:T(1024)S(1)}, bf16[1024,1536]{1,0:T(8,128)(2,1)S(1)}) fusion(f32[1024,1536]{1,0:T(8,128)} %get-tuple-element.63, f32[1536]{0:T(1024)S(1)} %copy-done.30, bf16[1536,768]{1,0:T(8,128)(2,1)} %all-gather.10.cloned.1.call-done, bf16[512,768]{1,0:T(8,128)(2,1)} %collective-permute-done.12, ...), kind=kOutput, calls=%fused_computation.9 | convolution fusion | flops 2455239168 | bytes 13381632 | tf_op jit(solution)/shard_map/dot_general | solution.py:38
  224.0 5.3 convolution_convert_fusion.1
  229.9 5.2 fusion.44
  249.1 6.2 %convolution_convert_fusion = bf16[1536,768]{1,0:T(8,128)(2,1)} fusion(bf16[1024,1536]{1,0:T(8,128)(2,1)} %get-tuple-element.62, bf16[512,768]{1,0:T(8,128)(2,1)} %collective-permute-done.12, bf16[512,768]{1,0:T(8,128)(2,1)S(1)} %get-tuple-element.37), kind=kOutput, calls=%fused_computation.13 | convolution fusion | flops 2420244480 | bytes 7077888 | tf_op jit(solution)/shard_map/dot_general | solution.py:42
  258.8 17.4 %attend_back.1 = bf16[1024,1152]{1,0:T(8,128)(2,1)} custom-call(s32[1]{0:T(128)} %bitcast.2.rank_ref, bf16[1024,1152]{1,0:T(8,128)(2,1)} %multiply_convert_fusion.1.qkv_ref, bf16[1024,384]{1,0:T(8,128)(2,1)} %convolution_convert_fusion.3.grad_ref, f32[3,2,1024]{2,1,0:T(2,128)} %get-tuple-element.13.log_ref), custom_call_target="tpu_custom_call" | custom-call | flops 8053063680 | bytes 5505024 | tf_op jit(solution)/shard_map/attend_back/pallas_call | solution.py:383
  276.2 4.2 convolution_convert_fusion.2
  286.3 26.5 %collective-permute-done.8 = bf16[256,768]{1,0:T(8,128)(2,1)S(1)} collective-permute-done((bf16[256,768]{1,0:T(8,128)(2,1)S(1)}, bf16[256,768]{1,0:T(8,128)(2,1)S(1)}, u32[]{:S(2)}, u32[]{:S(2)}) %collective-permute-start.8) | collective-permute-done | bytes 393248 | tf_op jit(solution)/shard_map/ppermute | solution.py:273
  312.9 25.3 %collective-permute-done.9 = bf16[256,768]{1,0:T(8,128)(2,1)S(1)} collective-permute-done((bf16[256,768]{1,0:T(8,128)(2,1)S(1)}, bf16[256,768]{1,0:T(8,128)(2,1)S(1)}, u32[]{:S(2)}, u32[]{:S(2)}) %collective-permute-start.9) | collective-permute-done | bytes 393248 | tf_op jit(solution)/shard_map/ppermute | solution.py:274
  339.2 4.6 fusion.46
  348.6 11.5 %reduce-scatter.9.cloned.1.call-done = bf16[96,768]{1,0:T(8,128)(2,1)} async-done(((bf16[384,768]{1,0:T(8,128)(2,1)}), bf16[96,768]{1,0:T(8,128)(2,1)}) %reduce-scatter.9.cloned.1.call-update) | async-done | bytes 147472 | tf_op jit(solution)/shard_map/reduce_scatter | solution.py:329
  360.1 49.8 %reduce-scatter.11.cloned.1.call-done = bf16[384,768]{1,0:T(8,128)(2,1)} async-done(((bf16[1536,768]{1,0:T(8,128)(2,1)}), bf16[384,768]{1,0:T(8,128)(2,1)}) %reduce-scatter.11.cloned.1.call-update) | async-done | bytes 589840 | tf_op jit(solution)/shard_map/reduce_scatter | solution.py:329
  409.9 40.8 %reduce-scatter.7.cloned.1.call-done = bf16[1,2,96,1152]{3,2,1,0:T(8,128)(2,1)} async-done(((bf16[4,2,96,1152]{3,2,1,0:T(8,128)(2,1)}), bf16[1,2,96,1152]{3,2,1,0:T(8,128)(2,1)}) %reduce-scatter.7.cloned.1.call-update) | async-done | bytes 442384 | tf_op jit(solution)/shard_map/reduce_scatter | solution.py:315
  455.8 5.0 collective-permute-start.16
  461.5 41.1 %all-reduce.1 = (f32[8,768]{1,0:T(8,128)S(1)}, f32[3072]{0:T(1024)S(1)}) all-reduce(f32[8,768]{1,0:T(8,128)S(1)} %stack.151, f32[3072]{0:T(1024)S(1)} %dynamic_update_slice.13), channel_id=1, replica_groups=mesh['replica'=4,'shard'=2,'ctx'=4] {'replica','shard','ctx'}, use_global_device_ids=true, to_apply=%region_23.24 | all-reduce | flops 9216 | bytes 73728 | tf_op jit(solution)/shard_map/psum | solution.py:413
  502.7 19.0 %all-reduce.8.cloned.1.call-done = (bf16[2,96,1152]{2,1,0:T(8,128)(2,1)}, bf16[96,768]{1,0:T(8,128)(2,1)}, bf16[2,96,1536]{2,1,0:T(8,128)(2,1)}, bf16[384,768]{1,0:T(8,128)(2,1)}) async-done(((bf16[2,96,1152]{2,1,0:T(8,128)(2,1)}, bf16[96,768]{1,0:T(8,128)(2,1)}, bf16[2,96,1536]{2,1,0:T(8,128)(2,1)}, bf16[384,768]{1,0:T(8,128)(2,1)}), (bf16[2,96,1152]{2,1,0:T(8,128)(2,1)}, bf16[96,768]{1,0:T(8,128)(2,1)}, ...) | async-done | bytes 1769488 | tf_op jit(solution)/shard_map/psum | solution.py:316
  (232 shorter events, 86.4 us)
Async XLA Ops:
  7.2 102.1 %all-gather.6.cloned.1.call-start = ((), (), s32[]{:S(2)}) async-start(), calls=%async_computation.3 | async-start | bytes 2211840 | tf_op jit(solution)/shard_map/all_gather | solution.py:297
  12.3 187.1 %all-gather.8.cloned.1.call-start = ((), (), s32[]{:S(2)}) async-start(), calls=%async_computation.4 | async-start | bytes 2949120 | tf_op jit(solution)/shard_map/all_gather | solution.py:297
  16.6 192.1 %all-gather.10.cloned.1.call-start = ((), (), s32[]{:S(2)}) async-start(), calls=%async_computation.5 | async-start | bytes 2949120 | tf_op jit(solution)/shard_map/all_gather | solution.py:305
  16.8 66.9 %collective-permute-start = (bf16[256,768]{1,0:T(8,128)(2,1)S(1)}, bf16[256,768]{1,0:T(8,128)(2,1)S(1)}, u32[]{:S(2)}, u32[]{:S(2)}) collective-permute-start(bf16[256,768]{1,0:T(8,128)(2,1)S(1)} %get-tuple-element.51), channel_id=1, source_target_pairs={{0,0},{1,1},{2,4},{3,5},{4,2},{5,3},{6,6},{7,7},{8,8},{9,9},{10,12... | collective-permute-start | bytes 1179656 | tf_op jit(solution)/shard_map/ppermute | solution.py:267
  21.3 62.4 %collective-permute-start.1 = (bf16[256,768]{1,0:T(8,128)(2,1)S(1)}, bf16[256,768]{1,0:T(8,128)(2,1)S(1)}, u32[]{:S(2)}, u32[]{:S(2)}) collective-permute-start(bf16[256,768]{1,0:T(8,128)(2,1)S(1)} %get-tuple-element.50), channel_id=1, source_target_pairs={{0,1},{1,0},{2,5},{3,4},{4,3},{5,2},{6,7},{7,6},{8,9},{9,8},{10,13... | collective-permute-start | bytes 1179656 | tf_op jit(solution)/shard_map/ppermute | solution.py:268
  84.8 24.5 %collective-permute-start.2 = (bf16[512,768]{1,0:T(8,128)(2,1)S(1)}, bf16[512,768]{1,0:T(8,128)(2,1)}, u32[]{:S(2)}, u32[]{:S(2)}) collective-permute-start(bf16[512,768]{1,0:T(8,128)(2,1)S(1)} %fusion.14), channel_id=1, source_target_pairs={{0,4},{1,5},{2,6},{3,7},{4,0},{5,1},{6,2},{7,3},{8,12},{9,13},{10,... | collective-permute-start | bytes 2359304 | tf_op jit(solution)/shard_map/ppermute | solution.py:278
  131.1 3.3 collective-permute-start.4
  132.6 213.4 %all-reduce.6.cloned.1.call-start = ((), (), s32[]{:S(2)}) async-start(), calls=%async_computation.9 | async-start | bytes 4718592
  137.9 61.5 %collective-permute-start.5 = (bf16[512,768]{1,0:T(8,128)(2,1)}, bf16[512,768]{1,0:T(8,128)(2,1)}, u32[]{:S(2)}, u32[]{:S(2)}) collective-permute-start(bf16[512,768]{1,0:T(8,128)(2,1)} %add_convert_fusion), channel_id=1, source_target_pairs={{0,4},{1,5},{2,6},{3,7},{4,0},{5,1},{6,2},{7,3},{8,12},{9,13},{10,... | collective-permute-start | bytes 2359304 | tf_op jit(solution)/shard_map/ppermute | solution.py:278
  138.3 34.2 %collective-permute-start.10 = (bf16[256,768]{1,0:T(8,128)(2,1)S(1)}, bf16[256,768]{1,0:T(8,128)(2,1)S(1)}, u32[]{:S(2)}, u32[]{:S(2)}) collective-permute-start(bf16[256,768]{1,0:T(8,128)(2,1)S(1)} %get-tuple-element.47), channel_id=1, source_target_pairs={{0,0},{1,1},{2,4},{3,5},{4,2},{5,3},{6,6},{7,7},{8,8},{9,9},{10,12... | collective-permute-start | bytes 1179656 | tf_op jit(solution)/shard_map/ppermute | solution.py:267
  142.9 54.5 %collective-permute-start.11 = (bf16[256,768]{1,0:T(8,128)(2,1)S(1)}, bf16[256,768]{1,0:T(8,128)(2,1)}, u32[]{:S(2)}, u32[]{:S(2)}) collective-permute-start(bf16[256,768]{1,0:T(8,128)(2,1)S(1)} %get-tuple-element.46), channel_id=1, source_target_pairs={{0,1},{1,0},{2,5},{3,4},{4,3},{5,2},{6,7},{7,6},{8,9},{9,8},{10,13... | collective-permute-start | bytes 1179656 | tf_op jit(solution)/shard_map/ppermute | solution.py:268
  199.4 9.4 %collective-permute-start.12 = (bf16[512,768]{1,0:T(8,128)(2,1)S(1)}, bf16[512,768]{1,0:T(8,128)(2,1)}, u32[]{:S(2)}, u32[]{:S(2)}) collective-permute-start(bf16[512,768]{1,0:T(8,128)(2,1)S(1)} %get-tuple-element.37), channel_id=1, source_target_pairs={{0,4},{1,5},{2,6},{3,7},{4,0},{5,1},{6,2},{7,3},{8,12},{9,13},{10,... | collective-permute-start | bytes 2359304 | tf_op jit(solution)/shard_map/ppermute | solution.py:278
  223.5 14.3 %collective-permute-start.13 = (bf16[512,768]{1,0:T(8,128)(2,1)}, bf16[512,768]{1,0:T(8,128)(2,1)}, u32[]{:S(2)}, u32[]{:S(2)}) collective-permute-start(bf16[512,768]{1,0:T(8,128)(2,1)} %slice.192), channel_id=1, source_target_pairs={{0,4},{1,5},{2,6},{3,7},{4,0},{5,1},{6,2},{7,3},{8,12},{9,13},{10,... | collective-permute-start | bytes 2359304 | tf_op jit(solution)/shard_map/ppermute | solution.py:284
  229.4 130.7 %reduce-scatter.9.cloned.1.call-start = ((), (), s32[]{:S(2)}) async-start(), calls=%async_computation.7 | async-start | bytes 737280 | tf_op jit(solution)/shard_map/reduce_scatter | solution.py:329
  249.1 160.8 %reduce-scatter.11.cloned.1.call-start = ((), (), s32[]{:S(2)}) async-start(), calls=%async_computation.8 | async-start | bytes 2949120 | tf_op jit(solution)/shard_map/reduce_scatter | solution.py:329
  255.4 195.3 %reduce-scatter.7.cloned.1.call-start = ((), (), s32[]{:S(2)}) async-start(), calls=%async_computation.6 | async-start | bytes 2211840 | tf_op jit(solution)/shard_map/reduce_scatter | solution.py:315
  281.8 240.0 %all-reduce.8.cloned.1.call-start = ((), (), s32[]{:S(2)}) async-start(), calls=%async_computation.10 | async-start | bytes 3538944 | tf_op jit(solution)/shard_map/psum | solution.py:316
  283.0 29.9 %collective-permute-start.8 = (bf16[256,768]{1,0:T(8,128)(2,1)S(1)}, bf16[256,768]{1,0:T(8,128)(2,1)S(1)}, u32[]{:S(2)}, u32[]{:S(2)}) collective-permute-start(bf16[256,768]{1,0:T(8,128)(2,1)S(1)} %get-tuple-element.48), channel_id=1, source_target_pairs={{0,0},{1,1},{4,2},{5,3},{2,4},{3,5},{6,6},{7,7},{8,8},{9,9},{12,10... | collective-permute-start | bytes 1179656 | tf_op jit(solution)/shard_map/ppermute | solution.py:273
  284.9 53.3 %collective-permute-start.9 = (bf16[256,768]{1,0:T(8,128)(2,1)S(1)}, bf16[256,768]{1,0:T(8,128)(2,1)S(1)}, u32[]{:S(2)}, u32[]{:S(2)}) collective-permute-start(bf16[256,768]{1,0:T(8,128)(2,1)S(1)} %get-tuple-element.49), channel_id=1, source_target_pairs={{1,0},{0,1},{5,2},{4,3},{3,4},{2,5},{7,6},{6,7},{9,8},{8,9},{13,10... | collective-permute-start | bytes 1179656 | tf_op jit(solution)/shard_map/ppermute | solution.py:274
  345.5 105.3 %collective-permute-start.15 = (bf16[512,768]{1,0:T(8,128)(2,1)S(1)}, bf16[512,768]{1,0:T(8,128)(2,1)S(1)}, u32[]{:S(2)}, u32[]{:S(2)}) collective-permute-start(bf16[512,768]{1,0:T(8,128)(2,1)S(1)} %slice.191), channel_id=1, source_target_pairs={{0,4},{1,5},{2,6},{3,7},{4,0},{5,1},{6,2},{7,3},{8,12},{9,13},{10,... | collective-permute-start | bytes 2359304 | tf_op jit(solution)/shard_map/ppermute | solution.py:284
  455.8 70.4 %collective-permute-start.16 = (bf16[256,768]{1,0:T(8,128)(2,1)S(1)}, bf16[256,768]{1,0:T(8,128)(2,1)S(1)}, u32[]{:S(2)}, u32[]{:S(2)}) collective-permute-start(bf16[256,768]{1,0:T(8,128)(2,1)S(1)} %get-tuple-element.44), channel_id=1, source_target_pairs={{0,0},{1,1},{4,2},{5,3},{2,4},{3,5},{6,6},{7,7},{8,8},{9,9},{12,10... | collective-permute-start | bytes 1179656 | tf_op jit(solution)/shard_map/ppermute | solution.py:273
  460.8 65.4 %collective-permute-start.17 = (bf16[256,768]{1,0:T(8,128)(2,1)S(1)}, bf16[256,768]{1,0:T(8,128)(2,1)}, u32[]{:S(2)}, u32[]{:S(2)}) collective-permute-start(bf16[256,768]{1,0:T(8,128)(2,1)S(1)} %get-tuple-element.45), channel_id=1, source_target_pairs={{1,0},{0,1},{5,2},{4,3},{3,4},{2,5},{7,6},{6,7},{9,8},{8,9},{13,10... | collective-permute-start | bytes 1179656 | tf_op jit(solution)/shard_map/ppermute | solution.py:274
  522.9 10.5 %collective-permute-start.19 = (bf16[96,1536]{1,0:T(8,128)(2,1)S(1)}, bf16[96,1536]{1,0:T(8,128)(2,1)}, u32[]{:S(2)}, u32[]{:S(2)}) collective-permute-start(bf16[96,1536]{1,0:T(8,128)(2,1)S(1)} %get-tuple-element.53), channel_id=1, source_target_pairs={{0,4},{4,0},{1,5},{5,1},{2,6},{6,2},{3,7},{7,3},{8,12},{12,8},{9,1... | collective-permute-start | bytes 884744 | tf_op jit(solution)/shard_map/ppermute | solution.py:288
  524.4 6.0 %collective-permute-start.18 = (bf16[96,1152]{1,0:T(8,128)(2,1)}, bf16[96,1152]{1,0:T(8,128)(2,1)}, u32[]{:S(2)}, u32[]{:S(2)}) collective-permute-start(bf16[96,1152]{1,0:T(8,128)(2,1)} %get-tuple-element.57), channel_id=1, source_target_pairs={{0,4},{4,0},{1,5},{5,1},{2,6},{6,2},{3,7},{7,3},{8,12},{12,8},{9,1... | collective-permute-start | bytes 663560 | tf_op jit(solution)/shard_map/ppermute | solution.py:288
  (44 other events, 348.8 us)
Sparse Core Ops, SparseCore 0:
  12.4 53.6 all-gather.5
  68.2 60.1 all-gather.7
  132.7 64.6 all-gather.9
  229.5 107.7 all-reduce.5
  339.5 20.5 reduce-scatter.8
  362.3 47.5 reduce-scatter.10
  412.2 38.4 reduce-scatter.6
  455.1 66.6 all-reduce.7

commit v2 on v1

--- a/solution.py
+++ b/solution.py
@@ -206,6 +206,106 @@
     return forward, backward
 
 
+class Slots:
+    def __init__(self, shapes, buffers, pieces):
+        self.shapes, self.buffers, self.pieces = shapes, buffers, pieces
+
+    def copies(self, where, buffers, arrays, move):
+        for buffer, index, parts in self.pieces(where):
+            for array, slot_rows, slot_columns, row, columns in parts:
+                one = buffers[buffer].at[(*index, pl.ds(*slot_rows), pl.ds(*slot_columns))]
+                two = arrays[array].at[pl.ds(pl.multiple_of(row, 16), slot_rows[1]), pl.ds(*columns)]
+                move(one, two)
+
+
+def slot_kernel(slots, inward, where_ref, *refs):
+    size = len(slots.buffers) if inward else len(slots.shapes)
+    arrays, buffers = (refs[size:], refs[:size]) if inward else (refs[:size], refs[size:])
+
+    def move(low, high):
+        source, target = (low, high) if inward else (high, low)
+        target[...] = source[...]
+
+    slots.copies([where_ref[i] for i in range(2)], buffers, arrays, move)
+
+
+def local_call(kernel, given, made, name, scalars=0):
+    size = 2 * sum(2 * one.size for one in made)
+    specs = [pl.BlockSpec(memory_space=pltpu.SMEM)] * scalars
+    return pl.pallas_call(
+        kernel,
+        in_specs=specs + [pl.BlockSpec(memory_space=pltpu.VMEM)] * given,
+        out_specs=[pl.BlockSpec(memory_space=pltpu.VMEM)] * len(made),
+        out_shape=made,
+        compiler_params=pltpu.CompilerParams(vmem_limit_bytes=40 * 2**20),
+        cost_estimate=pl.CostEstimate(flops=0, bytes_accessed=size, transcendentals=0),
+        name=name,
+    )
+
+
+def low_shape(*shape):
+    return jax.ShapeDtypeStruct(shape, BF)
+
+
+def slot_call(slots, inward, name):
+    arrays = [low_shape(*shape) for shape in slots.shapes]
+    buffers = [low_shape(*shape) for shape in slots.buffers]
+    given, made = (buffers, arrays) if inward else (arrays, buffers)
+    return local_call(functools.partial(slot_kernel, slots, inward), len(given), made, name, 1)
+
+
+def halves_kernel(both, first, second):
+    for j in range(first.shape[0]):
+        first[j], second[j] = both[j, 0], both[j, 1]
+
+
+def near_rows(where_ref, side, rows, far):
+    bit = where_ref[1] // 2 if side == 0 else where_ref[1] % 2
+    return pl.ds(pl.multiple_of((bit ^ far) * rows, 16), rows)
+
+
+def widen_kernel(where_ref, both, got_first, got_second, first, second):
+    rows = got_first.shape[1]
+    for side, (got, out) in enumerate(((got_first, first), (got_second, second))):
+        for j in range(4):
+            out[j, near_rows(where_ref, side, rows, 0), :] = both[j, side]
+            out[j, near_rows(where_ref, side, rows, 1), :] = got[j]
+
+
+def fold_kernel(where_ref, first, got_first, second, got_second, *made):
+    rows = made[0].shape[1]
+    for side, (keep, got) in enumerate(((first, got_first), (second, got_second))):
+        for far in range(2):
+            at = near_rows(where_ref, side, rows, far)
+            for j in range(4):
+                made[2 * side + far][j] = (keep[j, at, :].astype(F32) + got[j, at, :].astype(F32)).astype(BF)
+
+
+def pair_kernel(first, got_first, second, got_second, out):
+    for j in range(first.shape[0]):
+        out[j, 0] = (first[j].astype(F32) + got_first[j].astype(F32)).astype(BF)
+        out[j, 1] = (second[j].astype(F32) + got_second[j].astype(F32)).astype(BF)
+
+
+def stack_kernel(*refs):
+    for j, ref in enumerate(refs[:-1]):
+        refs[-1][j] = ref[...]
+
+
+def relay_kernel(to_x, to_y, for_y, for_x, out_x, out_y):
+    out_x[:2] = to_x[:2]
+    out_x[2:] = (to_x[2:].astype(F32) + for_x[...].astype(F32)).astype(BF)
+    out_y[:2] = (to_y[:2].astype(F32) + for_y[...].astype(F32)).astype(BF)
+    out_y[2:] = to_y[2:]
+
+
+def split_kernel(own, by_x, by_y, vectors, *made):
+    for j, out in enumerate(made):
+        columns = own.shape[2]
+        out[:, :columns] = (own[j].astype(F32) + by_x[j].astype(F32) + by_y[j].astype(F32)).astype(BF)
+        out[:, columns:] = vectors[...]
+
+
 def row_moves(shards, spans, seqs):
     chips = spans // (2 * seqs)
     moves = ([], [])
@@ -253,6 +353,7 @@
     part, ff_part = width // ranks, hidden // ranks
     blocks = shards * spans
     heads = HEADS // ranks
+    local = weight_qkv.shape[0]
     lanes = 2 * HEAD_DIM if heads % 2 == 0 else heads * HEAD_DIM
     groups = part // lanes
     scale = HEAD_DIM ** (-0.5)
@@ -261,11 +362,15 @@
     turns = group_moves(shards, spans, ranks)
     odd_span = ctx % 2
     odd_sequence = (ctx // chips) % 2
-    paired = shards == 2
-
-    def to_rows(items):
+    replicas = lax.axis_size("replica")
+    paired = shards == 2 and spans == 4 and replicas == 4 and ranks == 2
+
+    def row_parts(items):
         one = lax.ppermute(lax.dynamic_index_in_dim(items, odd_span, 0, False), LINE, moves[0])
         two = lax.ppermute(lax.dynamic_index_in_dim(items, 1 - odd_span, 0, False), LINE, moves[1])
+        return one, two
+
+    def to_rows(one, two):
         return jnp.where(odd_sequence == 0, jnp.concatenate([one, two]), jnp.concatenate([two, one]))
 
     def from_rows(low):
@@ -277,72 +382,199 @@
     def gather_rows(low):
         return jnp.concatenate([low] + [lax.ppermute(low, LINE, one) for one in turns])
 
-    def scatter_rows(partial):
-        total = partial[:rows]
+    def scatter_rows(items, product):
+        got = []
         for k, one in enumerate(turns):
-            sent = partial[(k + 1) * rows : (k + 2) * rows].astype(BF)
-            total = total + lax.ppermute(sent, LINE, one).astype(F32)
+            sent = product(items[(k + 1) * rows : (k + 2) * rows]).astype(BF)
+            got.append(lax.ppermute(sent, LINE, one))
+        total = product(items[:rows])
+        for one in got:
+            total = total + one.astype(F32)
         return total
 
     def swap(items):
         return lax.ppermute(items, "shard", [(0, 1), (1, 0)])
 
     def gather_columns(weight):
-        if not paired:
-            whole = lax.all_gather(weight, LINE, axis=0, tiled=True)
-            return lax.dynamic_index_in_dim(whole, rank, 1, False)
-        mine = lax.dynamic_index_in_dim(weight, core, 1, False)
-        other = swap(lax.dynamic_index_in_dim(weight, 1 - core, 1, False))
-        both = jnp.where(core == 0, jnp.stack([mine, other]), jnp.stack([other, mine]))
-        whole = lax.all_gather(both, "ctx", axis=1)
-        return whole.reshape(blocks * weight.shape[0], weight.shape[2])
+        whole = lax.all_gather(weight, LINE, axis=0, tiled=True)
+        return lax.dynamic_index_in_dim(whole, rank, 1, False)
 
     def gather_lines(weight):
-        if not paired:
-            whole = lax.all_gather(weight, LINE, axis=0, tiled=True)
-            size = whole.shape[0] // ranks
-            return lax.dynamic_slice_in_dim(whole, rank * size, size, 0)
-        return lax.all_gather(weight, "ctx", axis=0, tiled=True)
+        whole = lax.all_gather(weight, LINE, axis=0, tiled=True)
+        size = whole.shape[0] // ranks
+        return lax.dynamic_slice_in_dim(whole, rank * size, size, 0)
 
     def scatter_columns(grad):
-        low = grad.astype(BF)
-        if not paired:
-            whole = jnp.zeros((grad.shape[0], ranks, grad.shape[1]), BF)
-            whole = lax.dynamic_update_slice_in_dim(whole, low[:, None], rank, 1)
-            owned = lax.psum_scatter(whole, LINE, scatter_dimension=0, tiled=True)
-            return lax.psum(owned, "replica").astype(F32)
-        both = low.reshape(2, spans, -1, grad.shape[1]).swapaxes(0, 1)
-        owned = lax.psum_scatter(both, "ctx", scatter_dimension=0, tiled=True)[0]
-        owned = lax.psum(owned, "replica")
-        mine = lax.dynamic_index_in_dim(owned, core, 0, False)
-        other = swap(lax.dynamic_index_in_dim(owned, 1 - core, 0, False))
-        mine, other = mine.astype(F32), other.astype(F32)
-        return jnp.where(core == 0, jnp.stack([mine, other], 1), jnp.stack([other, mine], 1))
+        whole = jnp.zeros((grad.shape[0], ranks, grad.shape[1]), BF)
+        whole = lax.dynamic_update_slice_in_dim(whole, grad[:, None], rank, 1)
+        owned = lax.psum_scatter(whole, LINE, scatter_dimension=0, tiled=True)
+        return lax.psum(owned, "replica").astype(F32)
 
     def scatter_lines(grad):
-        low = grad.astype(BF)
-        if not paired:
-            whole = jnp.zeros((grad.shape[0] * ranks, grad.shape[1]), BF)
-            whole = lax.dynamic_update_slice_in_dim(whole, low, rank * grad.shape[0], 0)
-            owned = lax.psum_scatter(whole, LINE, scatter_dimension=0, tiled=True)
-        else:
-            owned = lax.psum_scatter(low, "ctx", scatter_dimension=0, tiled=True)
+        whole = jnp.zeros((grad.shape[0] * ranks, grad.shape[1]), BF)
+        whole = lax.dynamic_update_slice_in_dim(whole, grad, rank * grad.shape[0], 0)
+        owned = lax.psum_scatter(whole, LINE, scatter_dimension=0, tiled=True)
         return lax.psum(owned, "replica").astype(F32)
+
+    replica = lax.axis_index("replica")
+    where = jnp.stack([ctx, replica]).astype(jnp.int32)
+
+    def along_z(items, step):
+        return lax.ppermute(items, "ctx", [(i, i ^ step) for i in range(4)])
+
+    def across(items, step):
+        return lax.ppermute(items, "replica", [(i, i ^ step) for i in range(4)])
+
+    def after(items, *others):
+        return lax.optimization_barrier((items, others))[0] if paired else items
+
+    def z_moves(own):
+        return [along_z(own, step) for step in (1, 2, 3)]
+
+    def stacked(own, seen, name):
+        return local_call(stack_kernel, 4, [low_shape(4, *own.shape)], name)(own, *seen)[0]
+
+    def xy_moves(four):
+        return across(four, 1), across(four, 2)
+
+    def relay_parts(by_x, by_y):
+        return by_x[:2], by_y[2:]
+
+    def relays(for_y, for_x):
+        return across(for_y, 2), across(for_x, 1)
+
+    def relayed(buffers, got, name):
+        shape = low_shape(*buffers[0].shape)
+        return local_call(relay_kernel, 4, [shape] * 2, name)(buffers[1], buffers[2], *got)
+
+    def split(own, got, vectors, name):
+        shape = low_shape(own.shape[1], own.shape[2] + vectors.shape[1])
+        return local_call(split_kernel, 4, [shape] * 4, name)(own, *got, vectors)
+
+    def z_sum(own, got):
+        return (own.astype(F32) + got[0].astype(F32) + got[1].astype(F32) + got[2].astype(F32)).astype(BF)
+
+    def plus(a, b):
+        return (a.astype(F32) + b.astype(F32)).astype(BF)
+
+    def by_quarters(one, got):
+        one, by_x, by_y, by_both = [i.astype(F32) for i in (one, *got)]
+        quarters = []
+        for quarter in range(4):
+            step = replica ^ quarter
+            near = jnp.where(step == 0, one, by_x)
+            quarters.append(jnp.where(step < 2, near, jnp.where(step == 2, by_y, by_both)))
+        return quarters
+
+    bits = (replica % 2, replica // 2)
+
+    def of_core(weight, kinds, one_core):
+        size = weight.shape[1] // (kinds * ranks)
+        starts = [(kind * ranks + one_core) * size for kind in range(kinds)]
+        return jnp.concatenate([lax.dynamic_slice_in_dim(weight, at, size, 1) for at in starts], 1)
+
+    def by_halves(weight, kinds):
+        mine, other = of_core(weight, kinds, core), swap(of_core(weight, kinds, 1 - core))
+        blocks_of = jnp.where(core == 0, mine, other), jnp.where(core == 0, other, mine)
+        return [
+            lax.dynamic_slice_in_dim(one, bit * (local // 2), local // 2, 0) for one, bit in zip(blocks_of, bits)
+        ]
+
+    def by_quarter(weight, kinds):
+        mine, other = of_core(weight, kinds, core), swap(of_core(weight, kinds, 1 - core))
+        chosen = jnp.where(core == replica // 2, mine, other)
+        return lax.dynamic_slice_in_dim(chosen, (replica % 2) * (local // 2), local // 2, 0)
+
+    def to_shard(first, second):
+        mine, other = jnp.where(core == 0, first, second), jnp.where(core == 0, second, first)
+        other = swap(other.astype(BF)).astype(F32)
+        return jnp.where(core == 0, mine, other), jnp.where(core == 0, other, mine)
+
+    def slot_groups():
+        ff_local = weight_back.shape[0]
+        half, ff_half, wide = local // 2, ff_local // 2, 3 * part
+        third = width // 2
+
+        def attention_pieces(where):
+            for buffer, (step, first, count) in enumerate(((0, 0, 4), (1, 0, 4), (2, 0, 4), (3, 0, 2), (3, 2, 2))):
+                quarter = where[1] ^ step
+                for j in range(count):
+                    at = (where[0] ^ (first + j)) * local + (quarter % 2) * half
+                    column = pl.multiple_of((quarter // 2) * third, 128)
+                    parts = [(1, (0, half), (wide, third), at, (column, third))]
+                    for group in range(groups):
+                        for kind in range(3):
+                            low, high = kind * part + group * lanes, (3 * group + kind) * lanes
+                            row = (quarter // 2) * third + at
+                            parts.append((0, (0, half), (low, lanes), row, (high, lanes)))
+                    yield buffer, (j,), parts
+
+        def ff_parts(side, cut, z):
+            at = side * third + z * local + cut * half
+            row = z * ff_local + side * ff_half + cut * (ff_half // 2)
+            return (
+                (0, (0, half), (0, width), at, (0, width)),
+                (0, (half, half), (0, width), at, (width, width)),
+                (1, (2 * half, ff_half // 2), (0, width), row, (0, width)),
+            )
+
+        def ff_pieces(where):
+            for side, bit in enumerate((where[1] % 2, where[1] // 2)):
+                for z in range(4):
+                    yield 2 * side, (z,), ff_parts(side, bit, z)
+                    yield 2 * side + 1, (z,), ff_parts(side, 1 - bit, z)
+
+        attention = (half, wide + third)
+        feed = (2 * half + ff_half // 2, width)
+        shapes = [(width, ff_part), (ff_part, width)]
+        return (
+            Slots([(width, wide), (part, width)], [(n, *attention) for n in (4, 4, 4, 2, 2)], attention_pieces),
+            Slots(shapes, [(4, *feed)] * 4, ff_pieces),
+        )
 
     small_in = jnp.concatenate(
         [gains_in, shifts_in, biases_in, ff_bias_in.reshape(hidden // width, width // blocks)]
     )
-    small = lax.all_gather(small_in, LINE, axis=0).astype(F32)
+    if paired:
+        attention_slots, ff_slots = slot_groups()
+        half, third = local // 2, width // 2
+        small_near = swap(small_in)
+        lines = lax.dynamic_slice(weight_out, ((replica % 2) * half, (replica // 2) * third), (half, third))
+        own = jnp.concatenate([by_quarter(weight_qkv, 3), lines], 1)
+        seen = z_moves(own)
+        owns = []
+        ff_quarter = weight_back.shape[0] // 4
+        for side, one in enumerate(by_halves(after(weight_in, own), 1)):
+            at = (2 * side + bits[side]) * ff_quarter
+            lines = lax.dynamic_slice_in_dim(weight_back, at, ff_quarter, 0)
+            owns.append(jnp.where(bits[1 - side] == 0, jnp.concatenate([one[:, :width], one[:, width:]]), lines))
+        owns = jnp.stack(owns)
+        ff_own = lax.all_gather(owns, "ctx", axis=0)
+        seen_small = after(jnp.stack([small_in, small_near]), own)
+        seen_small = jnp.concatenate([seen_small] + [along_z(seen_small, step) for step in (1, 2, 3)])
+        four = stacked(own, after(seen, (owns, seen_small)), "stack_attention")
+        xy = xy_moves(four)
+        token_parts = after(row_parts(tokens), four)
+        pieces = relay_parts(*xy)
+        relay = relays(*pieces)
+        qkv_part, out_part = slot_call(attention_slots, True, "join_attention")(where, four, *xy, *relay)
+    else:
+        ordered = weight_qkv.reshape(local, 3, ranks, groups, lanes).transpose(0, 2, 3, 1, 4)
+        qkv_part = gather_columns(ordered.reshape(local, ranks, 3 * part))
+        out_part = gather_lines(weight_out)
+        in_part = gather_columns(weight_in.reshape(local, ranks, ff_part))
+        back_part = gather_lines(weight_back)
+        token_parts = row_parts(tokens)
+
+    if paired:
+        every = jnp.arange(8)
+        near = ctx ^ (every % 4)
+        small = jnp.take(seen_small, 2 * near + (core ^ (every // 4)), axis=0).astype(F32)
+    else:
+        small = lax.all_gather(small_in, LINE, axis=0).astype(F32)
     vectors = small[:, :8].swapaxes(0, 1).reshape(8, width)
     gains, shifts, biases = vectors[0:2], vectors[2:4], vectors[4:8]
     ff_bias = lax.dynamic_slice_in_dim(small[:, 8:].reshape(hidden), rank * ff_part, ff_part, 0)
-
-    local = weight_qkv.shape[0]
-    ordered = weight_qkv.reshape(local, 3, ranks, groups, lanes).transpose(0, 2, 3, 1, 4)
-    qkv_part = gather_columns(ordered.reshape(local, ranks, 3 * part))
-    out_part = gather_lines(weight_out)
-    in_part = gather_columns(weight_in.reshape(local, ranks, ff_part))
-    back_part = gather_lines(weight_back)
 
     def of_rank(vector):
         return lax.dynamic_slice_in_dim(vector, rank * part, part, 0).reshape(groups, lanes)
@@ -353,45 +585,83 @@
     attend, attend_back = attention_calls(length, rows, groups, lanes)
     rank_word = rank.astype(jnp.int32).reshape(1)
 
-    inputs = to_rows(tokens).astype(F32)
-    grad_low = to_rows(cotangent)
+    inputs = to_rows(*token_parts).astype(F32)
     normed_one, spread_one = normalize(inputs)
     first_all = gather_rows((normed_one * gains[0] + shifts[0]).astype(BF))
+    if paired:
+        quarters = [low_shape(4, *owns.shape[1:])] * 2
+        ff_near = local_call(halves_kernel, 1, quarters, "halves_ff")(after(ff_own, qkv_part))
+        ff_got = across(ff_near[0], 2), across(ff_near[1], 1)
+        first_all = after(first_all, ff_near)
     qkv = ((dot(first_all, qkv_part) + qkv_bias) * qkv_scale).astype(BF)
     mixed, logs = attend(rank_word, qkv)
-    hidden_in = inputs + scatter_rows(dot(mixed, out_part)) + biases[2]
+    if paired:
+        halves = [low_shape(4, 2 * owns.shape[1], width)] * 2
+        ff_near = local_call(widen_kernel, 3, halves, "widen_ff", 1)(where, ff_own, *after(ff_got, mixed))
+        ff_far = across(ff_near[0], 1), across(ff_near[1], 2)
+        mixed = after(mixed, ff_near)
+        cotangent = after(cotangent, ff_near)
+    cotangent_parts = row_parts(cotangent)
+    hidden_in = inputs + scatter_rows(mixed, lambda one: dot(one, out_part)) + biases[2]
     normed_two, spread_two = normalize(hidden_in)
-    second_all = gather_rows((normed_two * gains[1] + shifts[1]).astype(BF))
+    second = (normed_two * gains[1] + shifts[1]).astype(BF)
+    second_all = gather_rows(second)
+    if paired:
+        in_part, back_part = slot_call(ff_slots, True, "join_ff")(
+            where, ff_near[0], after(ff_far[0], second), ff_near[1], after(ff_far[1], second)
+        )
     inner = dot(second_all, in_part) + ff_bias
     active = jax.nn.gelu(inner).astype(BF)
-    result = hidden_in + scatter_rows(dot(active, back_part)) + biases[3]
+    grad_low = to_rows(*after(cotangent_parts, active))
+    result = hidden_in + scatter_rows(active, lambda one: dot(one, back_part)) + biases[3]
     output = from_rows(result.astype(BF))
 
     grad_rows = grad_low.astype(F32)
     grad_all = gather_rows(grad_low)
     grad_active = dot_nt(grad_all, back_part)
     grad_inner = jax.vjp(jax.nn.gelu, inner)[1](grad_active)[0].astype(BF)
-    grad_back = dot_tn(active, grad_all)
-    grad_in = dot_tn(second_all, grad_inner)
-    grad_second = scatter_rows(dot_nt(grad_inner, in_part))
+    grad_back = dot_tn(active, grad_all).astype(BF)
+    grad_in = dot_tn(second_all, grad_inner).astype(BF)
+    if paired:
+        ff_buffers = slot_call(ff_slots, False, "part_ff")(where, grad_in, grad_back)
+        ff_got = across(ff_buffers[1], 1), across(ff_buffers[3], 2)
+        grad_inner = after(grad_inner, ff_buffers)
+    grad_second = scatter_rows(grad_inner, lambda one: dot_nt(one, in_part))
     grad_hidden = grad_rows + norm_back(grad_second * gains[1], normed_two, spread_two)
 
     grad_branch = grad_hidden.astype(BF)
     branch_all = gather_rows(grad_branch)
     grad_mixed = dot_nt(branch_all, out_part).astype(BF)
-    grad_out = dot_tn(mixed, branch_all)
+    if paired:
+        ff_sums = local_call(fold_kernel, 4, quarters * 2, "fold_ff", 1)(
+            where, ff_buffers[0], *after((ff_got[0], ff_buffers[2], ff_got[1]), branch_all)
+        )
+        ff_got = across(ff_sums[1], 2), across(ff_sums[3], 1)
+        grad_mixed = after(grad_mixed, ff_sums)
     grad_qkv = attend_back(rank_word, qkv, grad_mixed, logs)
-    grad_first = scatter_rows(dot_nt(grad_qkv, qkv_part))
-    grad_weight = dot_tn(first_all, grad_qkv)
+    if paired:
+        ff_got = after(ff_got, (grad_qkv, output))
+        ff_sums = local_call(pair_kernel, 4, [low_shape(4, 2, *ff_sums[0].shape[1:])], "add_ff")(
+            ff_sums[0], ff_got[0], ff_sums[2], ff_got[1]
+        )[0]
+        grad_qkv = after(grad_qkv, ff_sums)
+        ff_one = lax.psum_scatter(
+            ff_sums.reshape(-1, width), "ctx", scatter_dimension=0, tiled=True
+        ).reshape(ff_sums.shape[1:])
+    grad_first = scatter_rows(grad_qkv, lambda one: dot_nt(one, qkv_part))
+    grad_out = dot_tn(mixed, branch_all).astype(BF)
+    grad_weight = dot_tn(first_all, grad_qkv).astype(BF)
+    if paired:
+        buffers = slot_call(attention_slots, False, "part_attention")(where, grad_weight, grad_out)
+        got = across(buffers[3], 1), across(buffers[4], 2)
+        grad_first = after(grad_first, buffers)
     grad_inputs = grad_hidden + norm_back(grad_first * gains[0], normed_one, spread_one)
-    grad_tokens = from_rows(grad_inputs.astype(BF))
-
-    owned_back = scatter_lines(grad_back)
-    owned_in = scatter_columns(grad_in).reshape(local, hidden)
-    owned_out = scatter_lines(grad_out)
-    owned_qkv = scatter_columns(grad_weight).reshape(local, ranks, groups, 3, lanes)
-    owned_qkv = owned_qkv.transpose(0, 3, 1, 2, 4).reshape(local, 3 * width)
-
+    grad_tokens_low = grad_inputs.astype(BF)
+    grad_tokens = from_rows(grad_tokens_low)
+
+    grad_second_late, grad_branch, grad_rows, grad_inner = after(
+        (grad_second, grad_branch, grad_rows, grad_inner), grad_weight
+    )
     qkv_sums = jnp.sum(grad_qkv.astype(F32), 0).reshape(groups, 3, lanes)
 
     def at_rank(vector, size):
@@ -400,20 +670,63 @@
     sums = jnp.stack(
         [
             jnp.sum(grad_first * normed_one, 0),
-            jnp.sum(grad_second * normed_two, 0),
+            jnp.sum(grad_second_late * normed_two, 0),
             jnp.sum(grad_first, 0),
-            jnp.sum(grad_second, 0),
+            jnp.sum(grad_second_late, 0),
             at_rank(qkv_sums[:, 0].reshape(part), width),
             at_rank(qkv_sums[:, 2].reshape(part), width),
             jnp.sum(grad_branch.astype(F32), 0),
             jnp.sum(grad_rows, 0),
         ]
     )
-    ff_sums = at_rank(jnp.sum(grad_inner.astype(F32), 0), hidden)
-    sums = lax.psum((sums, ff_sums), EVERY)
+    ff_sums_of = at_rank(jnp.sum(grad_inner.astype(F32), 0), hidden)
+    if paired:
+        wide = 3 * part
+        sent = relayed(buffers, after(got, grad_tokens_low), "relay_attention")
+        got = across(sent[0], 1), across(sent[1], 2)
+        vectors = jnp.concatenate([sums.reshape(-1), ff_sums_of.reshape(-1)]).astype(BF)
+        lane_block = 128 * (-(-vectors.size // (128 * (local // 2))))
+        vectors = jnp.pad(vectors, (0, lane_block * (local // 2) - vectors.size)).reshape(local // 2, lane_block)
+        parts = split(buffers[0], after(got, ff_one), vectors, "split_attention")
+        got = [along_z(parts[step], step) for step in (1, 2, 3)]
+        ff_got = across(ff_one[0], 2), across(ff_one[1], 1)
+        ff_halves = []
+        for bit, mine, other in zip(bits[::-1], ff_one, ff_got):
+            ff_halves.append(jnp.where(bit == 0, jnp.concatenate([mine, other]), jnp.concatenate([other, mine])))
+        ff_got = across(ff_halves[0], 1), across(ff_halves[1], 2)
+        ff_owned = []
+        for bit, mine, other in zip(bits, ff_halves, ff_got):
+            mine, other = mine.astype(F32), other.astype(F32)
+            ff_owned.append((jnp.where(bit == 0, mine, other), jnp.where(bit == 0, other, mine)))
+        one = z_sum(parts[0], after(got, (grad_tokens, ff_one)))
+        quarters = by_quarters(one, [across(one, step) for step in (1, 2, 3)])
+        vectors = [i[:, wide + third :] for i in quarters]
+        vectors = vectors[0] + vectors[1] + vectors[2] + vectors[3]
+        joined = [jnp.concatenate(quarters[:2]), jnp.concatenate(quarters[2:])]
+        owned_out = jnp.concatenate([one[:, wide : wide + third] for one in joined], 1)
+        low, high = to_shard(*[one[:, :wide] for one in joined])
+        owned_qkv = [i[:, kind * part : (kind + 1) * part] for kind in range(3) for i in (low, high)]
+        owned_qkv = jnp.concatenate(owned_qkv, 1)
+        half = local // 2
+        blocks_in = [
+            jnp.concatenate([jnp.concatenate([cut[:half], cut[half : 2 * half]], 1) for cut in one]) for one in ff_owned
+        ]
+        owned_in = jnp.concatenate(to_shard(*blocks_in), 1)
+        owned_back = jnp.concatenate([cut[2 * half :] for one in ff_owned for cut in one])
+    else:
+        owned_back, owned_in = scatter_lines(grad_back), scatter_columns(grad_in).reshape(local, hidden)
+        owned_out, owned_qkv = scatter_lines(grad_out), scatter_columns(grad_weight)
+        owned_qkv = owned_qkv.reshape(local, ranks, groups, 3, lanes)
+        owned_qkv = owned_qkv.transpose(0, 3, 1, 2, 4).reshape(local, 3 * width)
+
+    if paired:
+        total = (vectors + swap(vectors)).reshape(-1)
+        sums, ff_sums_of = total[: 8 * width].reshape(8, width), total[8 * width : 8 * width + hidden]
+    else:
+        sums, ff_sums_of = lax.psum((sums, ff_sums_of), EVERY)
     at = shard * spans + ctx
-    mine = lax.dynamic_slice_in_dim(sums[0], at * (width // blocks), width // blocks, 1)
-    ff_mine = lax.dynamic_slice_in_dim(sums[1], at * (hidden // blocks), hidden // blocks, 0)
+    mine = lax.dynamic_slice_in_dim(sums, at * (width // blocks), width // blocks, 1)
+    ff_mine = lax.dynamic_slice_in_dim(ff_sums_of, at * (hidden // blocks), hidden // blocks, 0)
     return (
         output,
         grad_tokens,

time: 553 us -> 347 us (0.63)
  waiting for transfers between devices: 228 us -> 97.9 us
  blocking collectives: 125 us -> 0 us
  starting transfers between devices: 26.1 us -> 64.9 us
  Pallas kernels: 29.8 us -> 39.8 us
  matrix products: 58.1 us -> 66.4 us
    reduce_scatter x3 -> x1, waiting for transfers between devices: 102 us -> 0.02 us  [body(): lax.psum_scatter(ff_sums.reshape(-1, width), 'ctx', scatter_dimension=0,...]
    all_gather x2 -> x0, blocking collectives: 84.1 us -> none  [the longest x1 61.4 us: body(): small = lax.all_gather(small_in, LINE, axis=0).astype(F32)]
    psum x1 -> x0, blocking collectives: 41.1 us -> none  [body(): sums = lax.psum((sums, ff_sums), EVERY)]
    ppermute x8 -> x40, starting transfers between devices: 12.8 us -> 42.3 us  [the longest x23 21 us: across(): return lax.ppermute(items, 'replica', [(i, i ^ step) for i in range(4)])]
    psum x1 -> x0, waiting for transfers between devices: 19 us -> none  [scatter_columns(): owned = lax.psum(owned, 'replica')]
    ppermute x8 -> x40, waiting for transfers between devices: 50.8 us -> 69.3 us  [the longest x23 35 us: across(): return lax.ppermute(items, 'replica', [(i, i ^ step) for i in range(4)])]
    ppermute x2, waiting for transfers between devices: 26.5 us -> 10 us  [from_rows(): lax.ppermute(lax.dynamic_index_in_dim(items, odd_sequence, 0, False), LIN...]
    ppermute x2, waiting for transfers between devices: 25.3 us -> 11.9 us  [from_rows(): lax.ppermute(lax.dynamic_index_in_dim(items, 1 - odd_sequence, 0, False),...]
  transfers between devices with their start and end apart: 28 -> 56, of which waited for: 12 -> 22; matrix products, arithmetic and copies ran while one was open for 17% -> 25% of each run, Pallas kernels for 5% -> 10%
where the time goes in v2:
time: 347 us; the launch traced here: 340 us
  waiting for transfers between devices  97.9 us (28%)
  matrix products  66.4 us (19%)
  starting transfers between devices  64.9 us (19%)
  Pallas kernels  39.8 us (11%)
  other arithmetic  28.4 us (8%)
  local copies, waits for them, and re-layouts  26.7 us (8%)
  between operations  15.6 us (4%)
    ppermute x23, waiting for transfers between devices, across(): return lax.ppermute(items, 'replica', [(i, i ^ step) for i in range(4)])  35 us
    ppermute x9, waiting for transfers between devices, along_z(): return lax.ppermute(items, 'ctx', [(i, i ^ step) for i in range(4)])  34 us
    dot_general x6, matrix products, dot(): return jnp.dot(a, b, preferred_element_type=F32)  31.4 us
    dot_general x6, matrix products, dot_nt(): lax.dot_general(a, b, (((1,), (1,)), ((), ())), preferred_element_type=F32)  22.2 us
    ppermute x23, starting transfers between devices, across(): return lax.ppermute(items, 'replica', [(i, i ^ step) for i in range(4)])  21 us
    pallas_call x1, Pallas kernels, body(): grad_qkv = attend_back(rank_word, qkv, grad_mixed, logs)  17.3 us
    dot_general x4, matrix products, dot_tn(): lax.dot_general(a, b, (((0,), (0,)), ((), ())), preferred_element_type=F32)  12.8 us
    pallas_call x1, Pallas kernels, body(): mixed, logs = attend(rank_word, qkv)  12.5 us
  transfers between devices with their start and end apart: 56, of which 22 were waited for; matrix products, arithmetic and copies ran while one was open for 25% of the time, Pallas kernels for 10%

profile of v2, /device:TPU:9, one launch (start us, length us, event | category | flops | bytes accessed | tf_op | source)
XLA Modules:
  0.0 339.8 jit_solution(308714057427022295)
XLA Ops:
  11.5 4.6 %collective-permute-start = (bf16[256,768]{1,0:T(8,128)(2,1)S(1)}, bf16[256,768]{1,0:T(8,128)(2,1)S(1)}, u32[]{:S(2)}, u32[]{:S(2)}) collective-permute-start(bf16[256,768]{1,0:T(8,128)(2,1)S(1)} %get-tuple-element.176), channel_id=1, source_target_pairs={{0,0},{1,1},{2,4},{3,5},{4,2},{5,3},{6,6},{7,7},{8,8},{9,9},{10,12... | collective-permute-start | bytes 1179656 | tf_op jit(solution)/shard_map/ppermute | solution.py:369
  20.8 9.6 %collective-permute-done.8 = bf16[2,12,96]{2,1,0:T(8,128)(2,1)S(1)} collective-permute-done((bf16[2,12,96]{2,1,0:T(8,128)(2,1)S(1)}, bf16[2,12,96]{2,1,0:T(8,128)(2,1)S(1)}, u32[]{:S(2)}, u32[]{:S(2)}) %collective-permute-start.8) | collective-permute-done | bytes 4640 | tf_op jit(solution)/shard_map/ppermute | solution.py:423
  30.5 5.2 %collective-permute-done.9 = bf16[2,12,96]{2,1,0:T(8,128)(2,1)S(1)} collective-permute-done((bf16[2,12,96]{2,1,0:T(8,128)(2,1)S(1)}, bf16[2,12,96]{2,1,0:T(8,128)(2,1)S(1)}, u32[]{:S(2)}, u32[]{:S(2)}) %collective-permute-start.9) | collective-permute-done | bytes 4640 | tf_op jit(solution)/shard_map/ppermute | solution.py:423
  42.3 5.7 %collective-permute-done.5.refs_3_ = bf16[48,1536]{1,0:T(8,128)(2,1)S(1)} collective-permute-done((bf16[48,1536]{1,0:T(8,128)(2,1)S(1)}, bf16[48,1536]{1,0:T(8,128)(2,1)S(1)}, u32[]{:S(2)}, u32[]{:S(2)}) %collective-permute-start.5) | collective-permute-done | bytes 147488 | tf_op jit(solution)/shard_map/ppermute | solution.py:423
  53.5 9.1 %collective-permute-done.12.refs_1_ = bf16[4,48,1536]{2,1,0:T(8,128)(2,1)S(1)} collective-permute-done((bf16[4,48,1536]{2,1,0:T(8,128)(2,1)S(1)}, bf16[4,48,1536]{2,1,0:T(8,128)(2,1)S(1)}, u32[]{:S(2)}, u32[]{:S(2)}) %collective-permute-start.12) | collective-permute-done | bytes 589856 | tf_op jit(solution)/shard_map/ppermute | solution.py:426
  74.8 4.5 %all-gather.3.cloned.1.call-done = bf16[8,96,768]{2,1,0:T(8,128)(2,1)} async-done(((bf16[2,96,768]{2,1,0:T(8,128)(2,1)}), bf16[8,96,768]{2,1,0:T(8,128)(2,1)}) %all-gather.3.cloned.1.call-update) | async-done | bytes 1179664 | tf_op jit(solution)/shard_map/all_gather | solution.py:552
  83.1 5.7 %multiply_convert_fusion.1.qkv_ref = bf16[1024,1152]{1,0:T(8,128)(2,1)} fusion(bf16[1024,768]{1,0:T(8,128)(2,1)} %pad_maximum_fusion, bf16[768,1152]{1,0:T(8,128)(2,1)} %copy-done.8, f32[1152]{0:T(1024)S(1)} %copy-done.47, f32[1152]{0:T(1024)S(1)} %add.330), kind=kOutput, calls=%fused_computation.13 | convolution fusion | flops 1815478272 | bytes 5710848 | tf_op jit(solution)/shard_map/dot_general | solution.py:34
  88.7 12.5 %attend.1 = (bf16[1024,384]{1,0:T(8,128)(2,1)}, f32[3,2,1024]{2,1,0:T(2,128)}) custom-call(s32[1]{0:T(128)} %bitcast.6.rank_ref, bf16[1024,1152]{1,0:T(8,128)(2,1)} %multiply_convert_fusion.1.qkv_ref), custom_call_target="tpu_custom_call" | custom-call | flops 3221225472 | bytes 3145728 | tf_op jit(solution)/shard_map/attend/pallas_call | solution.py:597
  121.9 12.5 %collective-permute-done.20.refs_1_ = bf16[4,192,768]{2,1,0:T(8,128)(2,1)S(1)} collective-permute-done((bf16[4,192,768]{2,1,0:T(8,128)(2,1)S(1)}, bf16[4,192,768]{2,1,0:T(8,128)(2,1)S(1)}, u32[]{:S(2)}, u32[]{:S(2)}) %collective-permute-start.20) | collective-permute-done | bytes 1179680 | tf_op jit(solution)/shard_map/ppermute | solution.py:426
  136.0 6.0 %multiply_convert_fusion = (bf16[1024,1536]{1,0:T(8,128)(2,1)S(1)}, f32[1024,1536]{1,0:T(8,128)S(1)}) fusion(f32[1536]{0:T(1024)S(1)} %dynamic_slice.100, bf16[768,1536]{1,0:T(8,128)(2,1)S(1)} %get-tuple-element.97, bf16[512,768]{1,0:T(8,128)(2,1)} %collective-permute-done.19, bf16[512,768]{1,0:T(8,128)(2,1)} %add_convert_fusion.1), kind=kOutput, calls=%fused_computation.11 | convolution fusion | flops 2434793472 | bytes 13375488 | tf_op jit(solution)/shard_map/dot_general | solution.py:34
  149.7 6.8 %fusion.6 = bf16[1024,1536]{1,0:T(8,128)(2,1)S(1)} fusion(f32[1024,1536]{1,0:T(8,128)S(1)} %get-tuple-element.214, f32[1536]{0:T(1024)S(1)} %dynamic_slice.100, bf16[1536,768]{1,0:T(8,128)(2,1)S(1)} %get-tuple-element.98, bf16[512,768]{1,0:T(8,128)(2,1)S(1)} %collective-permute-done.27, bf16[512,768]{1,0:T(8,128)(2,1)S(1)} %get-tuple-element.159), kind=kOutput, calls=%fused_computation.9 | convolution fusion | flops 2452094976 | bytes 13375488 | tf_op jit(solution)/shard_map/dot_general | solution.py:38
  156.5 5.4 %convolution_convert_fusion.1.refs_0_ = bf16[768,1536]{1,0:T(8,128)(2,1)S(1)} fusion(bf16[1024,1536]{1,0:T(8,128)(2,1)S(1)} %fusion.6, bf16[512,768]{1,0:T(8,128)(2,1)} %collective-permute-done.19, bf16[512,768]{1,0:T(8,128)(2,1)} %add_convert_fusion.1), kind=kOutput, calls=%fused_computation.15 | convolution fusion | flops 2420244480 | bytes 7077888 | tf_op jit(solution)/shard_map/dot_general | solution.py:42
  176.0 12.0 %fusion.77 = (bf16[512,768]{1,0:T(8,128)(2,1)}, f32[512,768]{1,0:T(8,128)}, bf16[512,768]{1,0:T(8,128)(2,1)S(1)}) fusion(f32[512]{0:T(512)S(1)} %broadcast_multiply_fusion.2, f32[512,768]{1,0:T(8,128)S(1)} %copy-done.11, f32[512]{0:T(512)S(1)} %broadcast_multiply_fusion.4, f32[512]{0:T(512)S(1)} %broadcast_multiply_fusion.3, ...), kind=kOutput, calls=%fused_computation.219 | convolution fusion | flops 1213857792 | bytes 11812864 | tf_op jit(solution)/shard_map/dot_general | solution.py:34
  190.6 4.3 %collective-permute-start.23 = (bf16[256,768]{1,0:T(8,128)(2,1)}, bf16[256,768]{1,0:T(8,128)(2,1)}, u32[]{:S(2)}, u32[]{:S(2)}) collective-permute-start(bf16[256,768]{1,0:T(8,128)(2,1)} %get-tuple-element.173), channel_id=1, source_target_pairs={{0,0},{1,1},{4,2},{5,3},{2,4},{3,5},{6,6},{7,7},{8,8},{9,9},{12,10... | collective-permute-start | bytes 1179656 | tf_op jit(solution)/shard_map/ppermute | solution.py:378
  194.9 4.1 %collective-permute-done.30.got_first = bf16[4,192,768]{2,1,0:T(8,128)(2,1)S(1)} collective-permute-done((bf16[4,192,768]{2,1,0:T(8,128)(2,1)}, bf16[4,192,768]{2,1,0:T(8,128)(2,1)S(1)}, u32[]{:S(2)}, u32[]{:S(2)}) %collective-permute-start.30) | collective-permute-done | bytes 1179680 | tf_op jit(solution)/shard_map/ppermute | solution.py:426
  202.4 5.9 %collective-permute-done.23 = bf16[256,768]{1,0:T(8,128)(2,1)} collective-permute-done((bf16[256,768]{1,0:T(8,128)(2,1)}, bf16[256,768]{1,0:T(8,128)(2,1)}, u32[]{:S(2)}, u32[]{:S(2)}) %collective-permute-start.23) | collective-permute-done | bytes 393248 | tf_op jit(solution)/shard_map/ppermute | solution.py:378
  216.2 17.3 %attend_back.1 = bf16[1024,1152]{1,0:T(8,128)(2,1)} custom-call(s32[1]{0:T(128)} %bitcast.6.rank_ref, bf16[1024,1152]{1,0:T(8,128)(2,1)} %multiply_convert_fusion.1.qkv_ref, bf16[1024,384]{1,0:T(8,128)(2,1)} %convolution_convert_fusion.3.grad_ref, f32[3,2,1024]{2,1,0:T(2,128)} %get-tuple-element.115.log_ref), custom_call_target="tpu_custom_call" | custom-call | flops 8053063680 | bytes 5505024 | tf_op jit(solution)/shard_map/attend_back/pallas_call | solution.py:641
  266.0 4.5 %collective-permute-start.35 = (bf16[256,768]{1,0:T(8,128)(2,1)S(1)}, bf16[256,768]{1,0:T(8,128)(2,1)}, u32[]{:S(2)}, u32[]{:S(2)}) collective-permute-start(bf16[256,768]{1,0:T(8,128)(2,1)S(1)} %get-tuple-element.169), channel_id=1, source_target_pairs={{0,0},{1,1},{4,2},{5,3},{2,4},{3,5},{6,6},{7,7},{8,8},{9,9},{12,10... | collective-permute-start | bytes 1179656 | tf_op jit(solution)/shard_map/ppermute | solution.py:378
  271.4 11.9 %collective-permute-done.36 = bf16[256,768]{1,0:T(8,128)(2,1)} collective-permute-done((bf16[256,768]{1,0:T(8,128)(2,1)}, bf16[256,768]{1,0:T(8,128)(2,1)}, u32[]{:S(2)}, u32[]{:S(2)}) %collective-permute-start.36) | collective-permute-done | bytes 393248 | tf_op jit(solution)/shard_map/ppermute | solution.py:379
  283.2 4.1 %collective-permute-done.35 = bf16[256,768]{1,0:T(8,128)(2,1)} collective-permute-done((bf16[256,768]{1,0:T(8,128)(2,1)S(1)}, bf16[256,768]{1,0:T(8,128)(2,1)}, u32[]{:S(2)}, u32[]{:S(2)}) %collective-permute-start.35) | collective-permute-done | bytes 393248 | tf_op jit(solution)/shard_map/ppermute | solution.py:378
  296.9 6.5 %collective-permute-done.42 = bf16[48,1792]{1,0:T(8,128)(2,1)S(1)} collective-permute-done((bf16[48,1792]{1,0:T(8,128)(2,1)S(1)}, bf16[48,1792]{1,0:T(8,128)(2,1)S(1)}, u32[]{:S(2)}, u32[]{:S(2)}) %collective-permute-start.42) | collective-permute-done | bytes 172064 | tf_op jit(solution)/shard_map/ppermute | solution.py:423
  303.5 6.8 %collective-permute-done.43 = bf16[48,1792]{1,0:T(8,128)(2,1)S(1)} collective-permute-done((bf16[48,1792]{1,0:T(8,128)(2,1)S(1)}, bf16[48,1792]{1,0:T(8,128)(2,1)S(1)}, u32[]{:S(2)}, u32[]{:S(2)}) %collective-permute-start.43) | collective-permute-done | bytes 172064 | tf_op jit(solution)/shard_map/ppermute | solution.py:423
  315.8 4.6 %collective-permute-done.46 = bf16[48,1792]{1,0:T(8,128)(2,1)S(1)} collective-permute-done((bf16[48,1792]{1,0:T(8,128)(2,1)S(1)}, bf16[48,1792]{1,0:T(8,128)(2,1)S(1)}, u32[]{:S(2)}, u32[]{:S(2)}) %collective-permute-start.46) | collective-permute-done | bytes 172064 | tf_op jit(solution)/shard_map/ppermute | solution.py:426
  320.7 4.3 %collective-permute-start.53 = (f32[48,256]{1,0:T(8,128)S(1)}, f32[48,256]{1,0:T(8,128)S(1)}, u32[]{:S(2)}, u32[]{:S(2)}) collective-permute-start(f32[48,256]{1,0:T(8,128)S(1)} %slice_add_fusion), channel_id=1, source_target_pairs={{0,4},{4,0},{1,5},{5,1},{2,6},{6,2},{3,7},{7,3},{8,12},{12,8},{9,1... | collective-permute-start | bytes 147464 | tf_op jit(solution)/shard_map/ppermute | solution.py:396
  (347 shorter events, 150.2 us)
Async XLA Ops:
  7.2 72.1 %all-gather.3.cloned.1.call-start = ((), (), s32[]{:S(2)}) async-start(), calls=%async_computation.2 | async-start | bytes 1474560 | tf_op jit(solution)/shard_map/all_gather | solution.py:552
  11.5 39.2 %collective-permute-start = (bf16[256,768]{1,0:T(8,128)(2,1)S(1)}, bf16[256,768]{1,0:T(8,128)(2,1)S(1)}, u32[]{:S(2)}, u32[]{:S(2)}) collective-permute-start(bf16[256,768]{1,0:T(8,128)(2,1)S(1)} %get-tuple-element.176), channel_id=1, source_target_pairs={{0,0},{1,1},{2,4},{3,5},{4,2},{5,3},{6,6},{7,7},{8,8},{9,9},{10,12... | collective-permute-start | bytes 1179656 | tf_op jit(solution)/shard_map/ppermute | solution.py:369
  16.0 34.7 %collective-permute-start.1 = (bf16[256,768]{1,0:T(8,128)(2,1)S(1)}, bf16[256,768]{1,0:T(8,128)(2,1)S(1)}, u32[]{:S(2)}, u32[]{:S(2)}) collective-permute-start(bf16[256,768]{1,0:T(8,128)(2,1)S(1)} %get-tuple-element.175), channel_id=1, source_target_pairs={{0,1},{1,0},{2,5},{3,4},{4,3},{5,2},{6,7},{7,6},{8,9},{9,8},{10,13... | collective-permute-start | bytes 1179656 | tf_op jit(solution)/shard_map/ppermute | solution.py:370
  19.3 19.7 %collective-permute-start.10 = (bf16[2,12,96]{2,1,0:T(8,128)(2,1)S(1)}, bf16[2,12,96]{2,1,0:T(8,128)(2,1)S(1)}, u32[]{:S(2)}, u32[]{:S(2)}) collective-permute-start(bf16[2,12,96]{2,1,0:T(8,128)(2,1)S(1)} %pad_maximum_fusion.15), channel_id=1, source_target_pairs={{0,3},{1,2},{2,1},{3,0},{4,7},{5,6},{6,5},{7,4},{8,11},{9,10},{10,... | collective-permute-start | bytes 13832 | tf_op jit(solution)/shard_map/ppermute | solution.py:423
  50.6 239.1 %reduce-scatter.2.cloned.1.call-start = ((), (), s32[]{:S(2)}) async-start(), calls=%async_computation.1 | async-start | bytes 1474560 | tf_op jit(solution)/shard_map/reduce_scatter | solution.py:648
  80.6 20.6 %collective-permute-start.16 = (bf16[4,96,768]{2,1,0:T(8,128)(2,1)S(1)}, bf16[4,96,768]{2,1,0:T(8,128)(2,1)S(1)}, u32[]{:S(2)}, u32[]{:S(2)}) collective-permute-start(bf16[4,96,768]{2,1,0:T(8,128)(2,1)S(1)} %get-tuple-element.85), channel_id=1, source_target_pairs={{0,16},{8,24},{16,0},{24,8},{1,17},{9,25},{17,1},{25,9},{2,18},{10... | collective-permute-start | bytes 1769480 | tf_op jit(solution)/shard_map/ppermute | solution.py:426
  81.9 19.4 %collective-permute-start.17 = (bf16[4,96,768]{2,1,0:T(8,128)(2,1)S(1)}, bf16[4,96,768]{2,1,0:T(8,128)(2,1)S(1)}, u32[]{:S(2)}, u32[]{:S(2)}) collective-permute-start(bf16[4,96,768]{2,1,0:T(8,128)(2,1)S(1)} %get-tuple-element.86), channel_id=1, source_target_pairs={{0,8},{8,0},{16,24},{24,16},{1,9},{9,1},{17,25},{25,17},{2,10},{10... | collective-permute-start | bytes 1769480 | tf_op jit(solution)/shard_map/ppermute | solution.py:426
  106.7 27.7 %collective-permute-start.20 = (bf16[4,192,768]{2,1,0:T(8,128)(2,1)S(1)}, bf16[4,192,768]{2,1,0:T(8,128)(2,1)S(1)}, u32[]{:S(2)}, u32[]{:S(2)}) collective-permute-start(bf16[4,192,768]{2,1,0:T(8,128)(2,1)S(1)} %get-tuple-element.91.refs_0_), channel_id=1, source_target_pairs={{0,8},{8,0},{16,24},{24,16},{1,9},{9,1},{17,25},{25,17},{2,10},{10... | collective-permute-start | bytes 3538952 | tf_op jit(solution)/shard_map/ppermute | solution.py:426
  107.0 27.4 %collective-permute-start.21 = (bf16[4,192,768]{2,1,0:T(8,128)(2,1)S(1)}, bf16[4,192,768]{2,1,0:T(8,128)(2,1)}, u32[]{:S(2)}, u32[]{:S(2)}) collective-permute-start(bf16[4,192,768]{2,1,0:T(8,128)(2,1)S(1)} %get-tuple-element.92.refs_2_), channel_id=1, source_target_pairs={{0,16},{8,24},{16,0},{24,8},{1,17},{9,25},{17,1},{25,9},{2,18},{10... | collective-permute-start | bytes 3538952 | tf_op jit(solution)/shard_map/ppermute | solution.py:426
  112.6 23.5 %collective-permute-start.19 = (bf16[512,768]{1,0:T(8,128)(2,1)}, bf16[512,768]{1,0:T(8,128)(2,1)}, u32[]{:S(2)}, u32[]{:S(2)}) collective-permute-start(bf16[512,768]{1,0:T(8,128)(2,1)} %add_convert_fusion.1), channel_id=1, source_target_pairs={{0,4},{1,5},{2,6},{3,7},{4,0},{5,1},{6,2},{7,3},{8,12},{9,13},{10,... | collective-permute-start | bytes 2359304 | tf_op jit(solution)/shard_map/ppermute | solution.py:383
  117.6 24.4 %collective-permute-start.25 = (bf16[256,768]{1,0:T(8,128)(2,1)S(1)}, bf16[256,768]{1,0:T(8,128)(2,1)S(1)}, u32[]{:S(2)}, u32[]{:S(2)}) collective-permute-start(bf16[256,768]{1,0:T(8,128)(2,1)S(1)} %get-tuple-element.172), channel_id=1, source_target_pairs={{0,0},{1,1},{2,4},{3,5},{4,2},{5,3},{6,6},{7,7},{8,8},{9,9},{10,12... | collective-permute-start | bytes 1179656 | tf_op jit(solution)/shard_map/ppermute | solution.py:369
  120.4 21.6 %collective-permute-start.26 = (bf16[256,768]{1,0:T(8,128)(2,1)S(1)}, bf16[256,768]{1,0:T(8,128)(2,1)S(1)}, u32[]{:S(2)}, u32[]{:S(2)}) collective-permute-start(bf16[256,768]{1,0:T(8,128)(2,1)S(1)} %get-tuple-element.171), channel_id=1, source_target_pairs={{0,1},{1,0},{2,5},{3,4},{4,3},{5,2},{6,7},{7,6},{8,9},{9,8},{10,13... | collective-permute-start | bytes 1179656 | tf_op jit(solution)/shard_map/ppermute | solution.py:370
  171.5 27.5 %collective-permute-start.30 = (bf16[4,192,768]{2,1,0:T(8,128)(2,1)}, bf16[4,192,768]{2,1,0:T(8,128)(2,1)S(1)}, u32[]{:S(2)}, u32[]{:S(2)}) collective-permute-start(bf16[4,192,768]{2,1,0:T(8,128)(2,1)} %get-tuple-element.103), channel_id=1, source_target_pairs={{0,8},{8,0},{16,24},{24,16},{1,9},{9,1},{17,25},{25,17},{2,10},{10... | collective-permute-start | bytes 3538952 | tf_op jit(solution)/shard_map/ppermute | solution.py:426
  172.7 27.2 %collective-permute-start.31 = (bf16[4,192,768]{2,1,0:T(8,128)(2,1)}, bf16[4,192,768]{2,1,0:T(8,128)(2,1)}, u32[]{:S(2)}, u32[]{:S(2)}) collective-permute-start(bf16[4,192,768]{2,1,0:T(8,128)(2,1)} %get-tuple-element.105), channel_id=1, source_target_pairs={{0,16},{8,24},{16,0},{24,8},{1,17},{9,25},{17,1},{25,9},{2,18},{10... | collective-permute-start | bytes 3538952 | tf_op jit(solution)/shard_map/ppermute | solution.py:426
  188.0 22.6 %collective-permute-start.29 = (bf16[512,768]{1,0:T(8,128)(2,1)}, bf16[512,768]{1,0:T(8,128)(2,1)}, u32[]{:S(2)}, u32[]{:S(2)}) collective-permute-start(bf16[512,768]{1,0:T(8,128)(2,1)} %get-tuple-element.132), channel_id=1, source_target_pairs={{0,4},{1,5},{2,6},{3,7},{4,0},{5,1},{6,2},{7,3},{8,12},{9,13},{10,... | collective-permute-start | bytes 2359304 | tf_op jit(solution)/shard_map/ppermute | solution.py:383
  201.8 31.8 %collective-permute-start.32 = (bf16[4,96,768]{2,1,0:T(8,128)(2,1)S(1)}, bf16[4,96,768]{2,1,0:T(8,128)(2,1)S(1)}, u32[]{:S(2)}, u32[]{:S(2)}) collective-permute-start(bf16[4,96,768]{2,1,0:T(8,128)(2,1)S(1)} %get-tuple-element.111), channel_id=1, source_target_pairs={{0,16},{8,24},{16,0},{24,8},{1,17},{9,25},{17,1},{25,9},{2,18},{10... | collective-permute-start | bytes 1769480 | tf_op jit(solution)/shard_map/ppermute | solution.py:426
  202.1 31.4 %collective-permute-start.33 = (bf16[4,96,768]{2,1,0:T(8,128)(2,1)S(1)}, bf16[4,96,768]{2,1,0:T(8,128)(2,1)S(1)}, u32[]{:S(2)}, u32[]{:S(2)}) collective-permute-start(bf16[4,96,768]{2,1,0:T(8,128)(2,1)S(1)} %get-tuple-element.113), channel_id=1, source_target_pairs={{0,8},{8,0},{16,24},{24,16},{1,9},{9,1},{17,25},{25,17},{2,10},{10... | collective-permute-start | bytes 1769480 | tf_op jit(solution)/shard_map/ppermute | solution.py:426
  242.2 18.5 %collective-permute-start.37 = (bf16[2,48,1536]{2,1,0:T(8,128)(2,1)S(1)}, bf16[2,48,1536]{2,1,0:T(8,128)(2,1)S(1)}, u32[]{:S(2)}, u32[]{:S(2)}) collective-permute-start(bf16[2,48,1536]{2,1,0:T(8,128)(2,1)S(1)} %get-tuple-element.122), channel_id=1, source_target_pairs={{0,8},{8,0},{16,24},{24,16},{1,9},{9,1},{17,25},{25,17},{2,10},{10... | collective-permute-start | bytes 884744 | tf_op jit(solution)/shard_map/ppermute | solution.py:426
  260.9 28.9 %collective-permute-start.39 = (bf16[4,48,1536]{2,1,0:T(8,128)(2,1)S(1)}, bf16[4,48,1536]{2,1,0:T(8,128)(2,1)S(1)}, u32[]{:S(2)}, u32[]{:S(2)}) collective-permute-start(bf16[4,48,1536]{2,1,0:T(8,128)(2,1)S(1)} %get-tuple-element.127), channel_id=1, source_target_pairs={{0,8},{8,0},{16,24},{24,16},{1,9},{9,1},{17,25},{25,17},{2,10},{10... | collective-permute-start | bytes 1769480 | tf_op jit(solution)/shard_map/ppermute | solution.py:426
  262.2 27.6 %collective-permute-start.40 = (bf16[4,48,1536]{2,1,0:T(8,128)(2,1)S(1)}, bf16[4,48,1536]{2,1,0:T(8,128)(2,1)S(1)}, u32[]{:S(2)}, u32[]{:S(2)}) collective-permute-start(bf16[4,48,1536]{2,1,0:T(8,128)(2,1)S(1)} %get-tuple-element.128), channel_id=1, source_target_pairs={{0,16},{8,24},{16,0},{24,8},{1,17},{9,25},{17,1},{25,9},{2,18},{10... | collective-permute-start | bytes 1769480 | tf_op jit(solution)/shard_map/ppermute | solution.py:426
  263.4 19.8 %collective-permute-start.36 = (bf16[256,768]{1,0:T(8,128)(2,1)}, bf16[256,768]{1,0:T(8,128)(2,1)}, u32[]{:S(2)}, u32[]{:S(2)}) collective-permute-start(bf16[256,768]{1,0:T(8,128)(2,1)} %get-tuple-element.170), channel_id=1, source_target_pairs={{1,0},{0,1},{5,2},{4,3},{3,4},{2,5},{7,6},{6,7},{9,8},{8,9},{13,10... | collective-permute-start | bytes 1179656 | tf_op jit(solution)/shard_map/ppermute | solution.py:379
  266.0 21.4 %collective-permute-start.35 = (bf16[256,768]{1,0:T(8,128)(2,1)S(1)}, bf16[256,768]{1,0:T(8,128)(2,1)}, u32[]{:S(2)}, u32[]{:S(2)}) collective-permute-start(bf16[256,768]{1,0:T(8,128)(2,1)S(1)} %get-tuple-element.169), channel_id=1, source_target_pairs={{0,0},{1,1},{4,2},{5,3},{2,4},{3,5},{6,6},{7,7},{8,8},{9,9},{12,10... | collective-permute-start | bytes 1179656 | tf_op jit(solution)/shard_map/ppermute | solution.py:378
  294.4 18.7 %collective-permute-start.50 = (bf16[96,768]{1,0:T(8,128)(2,1)S(1)}, bf16[96,768]{1,0:T(8,128)(2,1)S(1)}, u32[]{:S(2)}, u32[]{:S(2)}) collective-permute-start(bf16[96,768]{1,0:T(8,128)(2,1)S(1)} %get-tuple-element.202), channel_id=1, source_target_pairs={{0,8},{8,0},{16,24},{24,16},{1,9},{9,1},{17,25},{25,17},{2,10},{10... | collective-permute-start | bytes 442376 | tf_op jit(solution)/shard_map/ppermute | solution.py:426
  295.6 18.7 %collective-permute-start.48 = (bf16[96,768]{1,0:T(8,128)(2,1)S(1)}, bf16[96,768]{1,0:T(8,128)(2,1)S(1)}, u32[]{:S(2)}, u32[]{:S(2)}) collective-permute-start(bf16[96,768]{1,0:T(8,128)(2,1)S(1)} %get-tuple-element.201), channel_id=1, source_target_pairs={{0,16},{8,24},{16,0},{24,8},{1,17},{9,25},{17,1},{25,9},{2,18},{10... | collective-permute-start | bytes 442376 | tf_op jit(solution)/shard_map/ppermute | solution.py:426
  (82 other events, 595.1 us)
Sparse Core Ops, SparseCore 0:
  50.8 28.4 all-gather.2
  243.9 29.6 reduce-scatter.1
